TPU v7x, 512 devices: a whole 4x4x16 slice. The times are simulated.
512 devices in a mesh: gx: 32 (over x_hi, z), gy: 16 (over y, x_lo, core).
Axes of the slice: x: 4 (x_hi: 2, x_lo: 2; x = x_hi * 2 + x_lo), y: 4, z: 16, core: 2. Of those that a mesh axis runs over, the one named last changes fastest.
Arguments:
- basis: float32 [3, 524288, 128], P(None, ('gx', 'gy')), may hold values from -6 to 6
- sphere_box: int32 [524288], P(('gx', 'gy')), may hold values from 0 to 255
- sphere_type: int32 [524288], P(('gx', 'gy')), may hold values from 0 to 7
- near_offsets: int32 [9, 2], replicated, may hold values from -1 to 1, as said below
- near_mats: float32 [9, 128, 128], replicated, may hold values from -0.5 to 0.5
- up_mat: float32 [128, 128], replicated, may hold values from -0.03125 to 0.03125
- top_mat: float32 [128, 128], replicated, may hold values from -0.09375 to 0.09375
- tmats: float32 [8, 128, 128], replicated, may hold values from -0.125 to 0.125
- bloch_angle: float32 [2], replicated, may hold values from -3.140625 to 3.140625
Outputs:
- next_vector: float32 [524288, 128], P(('gx', 'gy'))
- hess_column: float32 [4], replicated
Inputs may be any that keep to these rules, and one draw needn't show every extreme that they name: `near_offsets`: the rows are the nine offsets with both entries in -1, 0, 1, each once.
All inputs are finite; a program needn't handle non-finite values.
Results may differ from a plain program's by a relative error of at most 0.0003.
Values sent between devices are 32-bit elements; how exact they have to be, the bound alone decides.
A program may use at most 64 MiB of HBM per device.

v0:
```python
import jax
import jax.numpy as jnp
from jax import lax
from jax.sharding import PartitionSpec as P

SD = 1024
LX = 16
LY = 16
KB = 3


HIGHEST = lax.Precision.HIGHEST
wave_number = 2.3


def extended(x, sides, width):
    for axis, dim in sides:
        size, length = (lax.axis_size(axis), x.shape[dim])
        up = [(i, (i + 1) % size) for i in range(size)]
        down = [(j, i) for i, j in up]
        last = lax.slice_in_dim(x, length - width, length, axis=dim)
        leading = lax.slice_in_dim(x, 0, width, axis=dim)
        before = lax.ppermute(last, axis, up)
        after = lax.ppermute(leading, axis, down)
        x = jnp.concatenate([before, x, after], axis=dim)
    return x


def product(left, right):
    return jnp.dot(left, right, precision=HIGHEST, preferred_element_type=jnp.float32)


def rotate_pairs(values, angle):
    half_size = values.shape[-1] // 2
    real_part = values[..., :half_size]
    imag_part = values[..., half_size:]
    cosine = jnp.cos(angle)[..., None]
    sine_part = jnp.sin(angle)[..., None]
    return jnp.concatenate(
        [cosine * real_part - sine_part * imag_part, sine_part * real_part + cosine * imag_part],
        axis=-1,
    )


def far_weights(target_x, target_y, source_x, source_y, grid_x, grid_y, bloch_angle):
    shift_x = (source_x[None, :] - target_x[:, None] + grid_x // 2) % grid_x - grid_x // 2
    shift_y = (source_y[None, :] - target_y[:, None] + grid_y // 2) % grid_y - grid_y // 2
    cross_x = (target_x[:, None] + shift_x - source_x[None, :]) // grid_x
    cross_y = (target_y[:, None] + shift_y - source_y[None, :]) // grid_y
    reach = jnp.maximum(jnp.abs(shift_x), jnp.abs(shift_y))
    distance = (shift_x * shift_x + shift_y * shift_y).astype(jnp.float32)
    radius = jnp.sqrt(jnp.maximum(distance, 1.0))
    weight = jnp.where(reach >= 2, 16.0 / radius, 0.0)
    angle = (
        wave_number * radius
        + cross_x.astype(jnp.float32) * bloch_angle[0]
        + cross_y.astype(jnp.float32) * bloch_angle[1]
    )
    return (weight * jnp.cos(angle), weight * jnp.sin(angle))


def complex_apply(far_cos, far_sin, sources):
    half_size = sources.shape[1] // 2
    real_in = sources[:, :half_size]
    imag_in = sources[:, half_size:]
    real_out = product(far_cos, real_in) - product(far_sin, imag_in)
    imag_out = product(far_sin, real_in) + product(far_cos, imag_in)
    return jnp.concatenate([real_out, imag_out], axis=1)


def quad_coords(rows, tiles_y):
    device = rows // 4
    quarter = rows % 4
    return (2 * (device // tiles_y) + quarter // 2, 2 * (device % tiles_y) + quarter % 2)


def on_device(
    basis, sphere_box, sphere_type, near_offsets, near_mats, up_mat, top_mat, tmats, bloch_angle
):
    vector = basis[KB - 1]
    coef = vector.shape[1]
    tiles_x = lax.axis_size("gx")
    tiles_y = lax.axis_size("gy")
    tile_row = lax.axis_index("gx")
    tile_col = lax.axis_index("gy")
    box_ids = jnp.arange(LX * LY, dtype=jnp.int32)
    member = (sphere_box[None, :] == box_ids[:, None]).astype(jnp.float32)
    leaf_mult = product(member, vector).reshape(LX, LY, coef)
    padded = extended(leaf_mult, (("gx", 0), ("gy", 1)), 1)
    rim_rows = jnp.arange(LX + 2, dtype=jnp.int32)
    rim_cols = jnp.arange(LY + 2, dtype=jnp.int32)
    cross_rows = jnp.where((rim_rows == 0) & (tile_row == 0), -1.0, 0.0) + jnp.where(
        (rim_rows == LX + 1) & (tile_row == tiles_x - 1), 1.0, 0.0
    )
    cross_cols = jnp.where((rim_cols == 0) & (tile_col == 0), -1.0, 0.0) + jnp.where(
        (rim_cols == LY + 1) & (tile_col == tiles_y - 1), 1.0, 0.0
    )
    padded = rotate_pairs(
        padded, cross_rows[:, None] * bloch_angle[0] + cross_cols[None, :] * bloch_angle[1]
    )

    def window(offset):
        start_zero = jnp.zeros((), jnp.int32)
        return lax.dynamic_slice(padded, (1 + offset[0], 1 + offset[1], start_zero), (LX, LY, coef))

    windows = jax.vmap(window)(near_offsets).reshape(near_offsets.shape[0], LX * LY, coef)
    near = jnp.einsum(
        "okc,ocd->kd", windows, near_mats, precision=HIGHEST, preferred_element_type=jnp.float32
    )
    quad_sum = leaf_mult.reshape(2, LX // 2, 2, LY // 2, coef).sum(axis=(1, 3)).reshape(4, coef)
    expansion = product(quad_sum, up_mat)
    quarter = jnp.arange(4, dtype=jnp.int32)
    grid_x = 2 * tiles_x
    grid_y = 2 * tiles_y
    own_x = 2 * tile_row + quarter // 2
    own_y = 2 * tile_col + quarter % 2
    piece = lax.all_gather(expansion, ("gx", "gy"), axis=0, tiled=True)
    rows = jnp.arange(piece.shape[0], dtype=jnp.int32)
    source_x, source_y = quad_coords(rows, tiles_y)
    far_cos, far_sin = far_weights(own_x, own_y, source_x, source_y, grid_x, grid_y, bloch_angle)
    far = complex_apply(far_cos, far_sin, piece)
    far_top = product(far, top_mat)
    local_field = (
        near.reshape(2, LX // 2, 2, LY // 2, coef) + far_top.reshape(2, 1, 2, 1, coef)
    ).reshape(LX * LY, coef)
    field = lax.dot_general(
        member,
        local_field,
        (((0,), (0,)), ((), ())),
        precision=HIGHEST,
        preferred_element_type=jnp.float32,
    )
    ntypes = tmats.shape[0]
    stacked = jnp.transpose(tmats, (1, 0, 2)).reshape(coef, ntypes * coef)
    every_type = product(field, stacked).reshape(field.shape[0], ntypes, coef)
    chosen = sphere_type[:, None] == jnp.arange(ntypes, dtype=jnp.int32)[None, :]
    scattered = jnp.sum(jnp.where(chosen[:, :, None], every_type, 0.0), axis=1)
    image = vector - scattered
    count = float(tiles_x * tiles_y * SD * coef)
    local_products = jnp.einsum("ksc,sc->k", basis, image, precision=HIGHEST)
    coeffs = lax.psum(local_products, ("gx", "gy")) / count
    reduced = image - jnp.einsum("k,ksc->sc", coeffs, basis, precision=HIGHEST)
    square = lax.psum(jnp.sum(reduced * reduced), ("gx", "gy")) / count
    beta = jnp.sqrt(square + 1e-06)
    return (reduced / beta, jnp.concatenate([coeffs, beta[None]]))


def solution(mesh):
    return jax.shard_map(
        on_device,
        mesh=mesh,
        in_specs=(
            P(None, ("gx", "gy"), None),
            P(("gx", "gy")),
            P(("gx", "gy")),
            P(),
            P(),
            P(),
            P(),
            P(),
            P(),
        ),
        out_specs=(P(("gx", "gy"), None), P()),
        check_vma=False,
    )
```

profile of v0, /device:TPU:1, one launch (start us, length us, event | category | flops | bytes accessed | tf_op | source)
XLA Modules:
  0.0 1005.6 jit_solution(11899608526292945312)
XLA Ops:
  7.2 1.8 fusion.2
  9.0 4.4 collective-permute-start
  13.4 12.0 %collective-permute-start.1 = (f32[1,16,128]{2,1,0:T(8,128)S(1)}, f32[1,16,128]{2,1,0:T(8,128)S(1)}, u32[]{:S(2)}, u32[]{:S(2)}) collective-permute-start(f32[1,16,128]{2,1,0:T(8,128)S(1)} %get-tuple-element.25), channel_id=1, source_target_pairs={{16,0},{32,16},{48,32},{64,48},{80,64},{96,80},{112,96},{128,112},... | collective-permute-start | bytes 24584 | tf_op jit(solution)/shard_map/ppermute | solution.py:24
  25.4 1.6 convolution_bitcast_fusion.1
  27.0 1.3 fusion.134
  28.4 0.8 compare_select_fusion.1
  29.1 0.7 iota_compare_fusion.3
  29.8 1.3 fusion.62
  31.3 3.1 collective-permute-start.2
  34.4 1.9 collective-permute-start.3
  36.3 1.2 copy.19
  37.6 1.8 collective-permute-done.3
  39.4 0.2 multiply_subtract_fusion
  39.8 17.4 %while.1 = (s32[]{:T(128)}, f32[18,18,128]{2,1,0:T(8,128)S(1)}, s32[9,3]{0,1:T(4,128)S(1)}, f32[9,16,16,128]{3,2,1,0:T(8,128)S(1)}, s32[]{:T(128)}) while((s32[]{:T(128)}, f32[18,18,128]{2,1,0:T(8,128)S(1)}, s32[9,3]{0,1:T(4,128)S(1)}, f32[9,16,16,128]{3,2,1,0:T(8,128)S(1)}, s32[]{:T(128)}) %tuple.32), condition=%wide.while_cond, body=%wide.while_body.sunk | while | flops 2 | bytes 262261 | solution.py:104
  39.9 0.6 fusion.142
  40.4 1.3 bitcast_dynamic-update-slice_fusion.2
  41.8 0.6 fusion.142
  42.4 1.3 bitcast_dynamic-update-slice_fusion.2
  43.7 0.6 fusion.142
  44.3 1.3 bitcast_dynamic-update-slice_fusion.2
  45.7 0.6 fusion.142
  46.3 1.3 bitcast_dynamic-update-slice_fusion.2
  47.6 0.6 fusion.142
  48.2 1.3 bitcast_dynamic-update-slice_fusion.2
  49.6 0.6 fusion.142
  50.1 1.3 bitcast_dynamic-update-slice_fusion.2
  51.5 0.6 fusion.142
  52.1 1.3 bitcast_dynamic-update-slice_fusion.2
  53.4 0.6 fusion.142
  54.0 1.3 bitcast_dynamic-update-slice_fusion.2
  55.4 0.6 fusion.142
  55.9 1.3 bitcast_dynamic-update-slice_fusion.2
  57.2 1.1 fusion.9
  58.4 714.1 %all-gather.3.cloned.1.call-done = f32[512,4,128]{2,1,0:T(4,128)} async-done(((f32[1,4,128]{2,1,0:T(4,128)}), f32[512,4,128]{2,1,0:T(4,128)}) %all-gather.3.cloned.1.call-update) | async-done | bytes 1048592 | tf_op jit(solution)/shard_map/all_gather | solution.py:117
  772.4 3.6 fusion.5
  776.1 2.3 fusion.7
  778.4 2.5 convolution_add_fusion
  780.9 2.5 convolution_subtract_fusion
  783.4 0.2 fusion.53
  783.7 1.0 convolution_bitcast_fusion
  784.7 4.0 select_reduce_fusion
  788.8 0.3 multiply_reduce_fusion
  789.1 100.8 %psum.14 = f32[3]{0:T(128)S(1)} all-reduce(f32[3]{0:T(128)S(1)} %multiply_reduce_fusion), channel_id=1, replica_groups=mesh['gx'=32,'gy'=16] {'gx','gy'}, use_global_device_ids=true, to_apply=%region_2.3 | all-reduce | flops 3 | bytes 24 | tf_op jit(solution)/shard_map/psum | solution.py:141
  889.9 7.3 fusion
  897.2 0.7 multiply_reduce_fusion.1
  898.0 98.6 %psum.15 = f32[]{:T(128)} all-reduce(f32[]{:T(128)} %multiply_reduce_fusion.1), channel_id=1, replica_groups=mesh['gx'=32,'gy'=16] {'gx','gy'}, use_global_device_ids=true, to_apply=%region_4.5 | all-reduce | flops 1 | bytes 8 | tf_op jit(solution)/shard_map/psum | solution.py:143
  997.3 0.9 broadcast_divide_fusion
  998.2 0.6 pad_maximum_fusion.5
  (40 shorter events, 1.2 us)
Async XLA Ops:
  7.2 50.1 %copy-start = (f32[9,128,128]{2,1,0:T(8,128)S(1)}, f32[9,128,128]{2,1,0:T(8,128)}, u32[]{:S(2)}) copy-start(f32[9,128,128]{2,1,0:T(8,128)} %param.13) | copy-start | bytes 1769476
  7.2 765.3 %all-gather.3.cloned.1.call-start = ((), (), s32[]{:S(2)}) async-start(), calls=%async_computation | async-start | bytes 1050624 | tf_op jit(solution)/shard_map/all_gather | solution.py:117
  9.0 22.2 %collective-permute-start = (f32[1,16,128]{2,1,0:T(8,128)S(1)}, f32[1,16,128]{2,1,0:T(8,128)S(1)}, u32[]{:S(2)}, u32[]{:S(2)}) collective-permute-start(f32[1,16,128]{2,1,0:T(8,128)S(1)} %get-tuple-element.24), channel_id=1, source_target_pairs={{0,16},{16,32},{32,48},{48,64},{64,80},{80,96},{96,112},{112,128},... | collective-permute-start | bytes 24584 | tf_op jit(solution)/shard_map/ppermute | solution.py:23
  13.4 17.9 %collective-permute-start.1 = (f32[1,16,128]{2,1,0:T(8,128)S(1)}, f32[1,16,128]{2,1,0:T(8,128)S(1)}, u32[]{:S(2)}, u32[]{:S(2)}) collective-permute-start(f32[1,16,128]{2,1,0:T(8,128)S(1)} %get-tuple-element.25), channel_id=1, source_target_pairs={{16,0},{32,16},{48,32},{64,48},{80,64},{96,80},{112,96},{128,112},... | collective-permute-start | bytes 24584 | tf_op jit(solution)/shard_map/ppermute | solution.py:24
  31.3 6.3 collective-permute-start.2
  34.4 5.0 collective-permute-start.3
  772.4 3.6 copy-start.4
  778.4 5.0 copy-start.2
  780.9 2.8 copy-start.3
  784.7 4.1 copy-start.1
Sparse Core Ops, SparseCore 0:
  27.1 745.2 all-gather.2
where the time goes:
time: 1010 us
  waiting for transfers between devices  716 us (71%)
  blocking collectives  199 us (20%)
  matrix products  28 us (3%)
  starting transfers between devices  21.4 us (2%)
  local copies, waits for them, and re-layouts  19.9 us (2%)
  between operations  15 us (1%)
    all_gather x1, waiting for transfers between devices, on_device(): piece = lax.all_gather(expansion, ('gx', 'gy'), axis=0, tiled=True)  714 us
    psum x1, blocking collectives, on_device(): coeffs = lax.psum(local_products, ('gx', 'gy')) / count  101 us
    psum x1, blocking collectives, on_device(): square = lax.psum(jnp.sum(reduced * reduced), ('gx', 'gy')) / count  98.6 us
  transfers between devices with their start and end apart: 5, of which 2 were waited for; matrix products, arithmetic and copies ran while one was open for 3% of the time, Pallas kernels for 0%

commit v1 on v0

v1 whole, which is shorter than its diff:
```python
import functools

import jax
import jax.numpy as jnp
from jax import lax
from jax.experimental import pallas as pl
from jax.experimental.pallas import tpu as pltpu
from jax.sharding import PartitionSpec as P

SD = 1024
LX = 16
LY = 16
KB = 3
COEF = 128
NTYPE = 8
NOFF = 9
BOXES = LX * LY
CHUNK = 256

MESH = pl.DeviceIdType.MESH
wave_number = 2.3
f32 = jnp.float32
bf16 = jnp.bfloat16
i32 = jnp.int32


def iota(shape, dim):
    return lax.broadcasted_iota(i32, shape, dim)


def split(x):
    high = x.astype(bf16)
    return high, (x - high.astype(f32)).astype(bf16)


def dot(a, b):
    return jnp.dot(a, b, preferred_element_type=f32)


def ones_where(mask):
    return jnp.where(mask, 1.0, 0.0).astype(bf16)


def times_i(x):
    turned = pltpu.roll(x, COEF // 2, x.ndim - 1)
    return jnp.where(iota(x.shape, x.ndim - 1) < COEF // 2, -turned, turned)


def total_lane(x, lane):
    return jnp.sum(jnp.where(iota(x.shape, 1) == lane, x, 0.0), axis=1, keepdims=True)


def to_lanes(parts):
    rows = [jnp.sum(p, axis=0, keepdims=True) for p in parts]
    rows += [jnp.zeros((8 - len(rows), COEF), f32)]
    sums = jnp.sum(jnp.concatenate(rows, axis=0), axis=1, keepdims=True)
    placed = jnp.where(iota((8, COEF), 0) == iota((8, COEF), 1), sums, 0.0)
    return jnp.sum(placed, axis=0, keepdims=True)


def fold(x):
    return jnp.sum(x.reshape(x.shape[0] // 8, 8, COEF), axis=0)


def far_weights(nx, ny, gx, gy, theta):
    shape = (4 * ny, 8 * nx)
    m, n = iota(shape, 0), iota(shape, 1)
    grid_x, grid_y = 2 * nx, 2 * ny
    target_x, target_y = 2 * gx + ((m >> 1) & 1), 2 * (m >> 2) + (m & 1)
    source_x, source_y = 2 * (n >> 3) + ((n >> 1) & 1), 2 * gy + (n & 1)
    shift_x = ((source_x - target_x + grid_x // 2) & (grid_x - 1)) - grid_x // 2
    shift_y = ((source_y - target_y + grid_y // 2) & (grid_y - 1)) - grid_y // 2
    wraps_x, wraps_y = target_x + shift_x - source_x, target_y + shift_y - source_y
    cross_x = jnp.where(wraps_x > 0, 1.0, jnp.where(wraps_x < 0, -1.0, 0.0))
    cross_y = jnp.where(wraps_y > 0, 1.0, jnp.where(wraps_y < 0, -1.0, 0.0))
    reach = jnp.maximum(jnp.abs(shift_x), jnp.abs(shift_y))
    distance = (shift_x * shift_x + shift_y * shift_y).astype(f32)
    radius = jnp.sqrt(jnp.maximum(distance, 1.0))
    weight = jnp.where(reach >= 2, 16.0 / radius, 0.0)
    angle = wave_number * radius + cross_x * theta[0] + cross_y * theta[1]
    return weight * jnp.where((n & 4) == 0, jnp.cos(angle), jnp.sin(angle))


def kernel(
    nx, ny,
    basis_in, box_in, type_in, offsets_in, near_in, up_in, top_in, tmats_in, bloch_in,
    out_ref, hess_ref,
    basis, box, kind, offsets, near_mats, up, top, tmats, bloch,
    ebuf, gbuf, pbuf, rbuf, abuf, bbuf,
    edges, corners, rim, rim_corners, pad, far_w, top_t, hot, member_t, image, field,
    load_sem, e_sem, g_sem, r_sem, a_sem, b_sem, h_send, h_recv, out_sem,
):
    gx, gy = lax.axis_index("gx"), lax.axis_index("gy")
    count = float(nx * ny * SD * COEF)

    def load(src, dst, i):
        copy = pltpu.make_async_copy(src, dst, load_sem.at[i])
        copy.start()
        return copy

    load_vec = load(basis_in.at[KB - 1], basis.at[KB - 1], 0)
    load_box = load(box_in, box, 1)
    load_up = load(up_in, up, 2)
    load_bloch = load(bloch_in, bloch, 3)
    load_basis = load(basis_in.at[pl.ds(0, KB - 1)], basis.at[pl.ds(0, KB - 1)], 4)
    load_type = load(type_in, kind, 5)
    load_offsets = load(offsets_in, offsets, 6)
    load_near = load(near_in, near_mats, 7)
    load_top = load(top_in, top, 8)
    load_tmats = load(tmats_in, tmats, 9)

    barrier = pltpu.get_barrier_semaphore()

    def greet_x(k, c):
        pl.semaphore_signal(barrier, inc=1, device_id={"gx": (gx + k) % nx}, device_id_type=MESH)
        return c

    def greet_y(k, c):
        pl.semaphore_signal(barrier, inc=1, device_id={"gy": (gy + k) % ny}, device_id_type=MESH)
        return c

    lax.fori_loop(1, nx, greet_x, 0)
    lax.fori_loop(1, ny, greet_y, 0)
    sides = [(-1, 0), (1, 0), (0, -1), (0, 1), (-1, -1), (-1, 1), (1, -1), (1, 1)]

    def beside(side):
        return {"gx": (gx + side[0] + nx) % nx, "gy": (gy + side[1] + ny) % ny}

    for side in sides[4:]:
        pl.semaphore_signal(barrier, inc=1, device_id=beside(side), device_id_type=MESH)

    def send_x(buf, sem, rows):
        def body(k, c):
            near_half = nx // 2 + ((k + 1) // 2) * (1 - 2 * (k % 2))
            peer = (gx + near_half) % nx
            spot = buf.at[gx, pl.ds(0, rows)]
            pltpu.make_async_remote_copy(
                spot, spot, sem.at[0], sem.at[1], device_id={"gx": peer}, device_id_type=MESH
            ).start()
            return c

        lax.fori_loop(0, nx - 1, body, 0)

    def send_y(src, dst, sem, rows, scatter):
        def body(k, c):
            peer = (gy + k) % ny
            pltpu.make_async_remote_copy(
                src.at[peer if scatter else gy, pl.ds(0, rows)],
                dst.at[gy, pl.ds(0, rows)],
                sem.at[0], sem.at[1], device_id={"gy": peer}, device_id_type=MESH,
            ).start()
            return c

        lax.fori_loop(1, ny, body, 0)

    def wait_all(buf, sem, number, rows):
        span = buf.at[pl.ds(0, number), pl.ds(0, rows)]
        pltpu.make_async_copy(span, span, sem).wait()

    load_box.wait()
    boxes = box[...]
    member = jnp.concatenate(
        [ones_where(iota((BOXES, COEF), 0) == boxes[r : r + 1, :]) for r in range(SD // COEF)], axis=1
    )
    load_vec.wait()
    leaf2 = dot(member, jnp.concatenate(split(basis[KB - 1]), axis=1))
    leaf = (leaf2[:, :COEF] + leaf2[:, COEF:]).reshape(LX, LY, COEF)

    quads = []
    for a in range(2):
        for b in range(2):
            part = jnp.sum(leaf[a * 8 : a * 8 + 8, b * 8 : b * 8 + 8, :], axis=0)
            quads.append(jnp.sum(part, axis=0, keepdims=True))
    quad_sum = jnp.concatenate(quads + [jnp.zeros((4, COEF), f32)], axis=0)
    load_up.wait()
    quad_high, quad_low = split(quad_sum)
    pair = jnp.concatenate([quad_high.astype(f32), quad_low.astype(f32)], axis=0).astype(bf16)
    up_high, up_low = split(up[...])
    raised = dot(pair, up_high) + dot(pair, up_low)
    ebuf[gx, 0:4, :] = (raised[0:8] + raised[8:16])[0:4]
    pl.semaphore_wait(barrier, nx + ny + 2)
    send_x(ebuf, e_sem, 4)

    edges[0] = leaf[0]
    edges[1] = leaf[LX - 1]
    edges[2] = leaf[:, 0, :]
    edges[3] = leaf[:, LY - 1, :]
    for c, (x, y) in enumerate([(0, 0), (0, LY - 1), (LX - 1, 0), (LX - 1, LY - 1)]):
        corners[c, 0:1, :] = leaf[x, y : y + 1, :]
    halo = []
    for i, side in enumerate(sides):
        other = sides.index((-side[0], -side[1]))
        if i < 4:
            src, dst = edges.at[i], rim.at[other]
        else:
            src, dst = corners.at[i - 4], rim_corners.at[other - 4]
        copy = pltpu.make_async_remote_copy(
            src, dst, h_send.at[i], h_recv.at[other], device_id=beside(side), device_id_type=MESH
        )
        copy.start()
        halo.append(copy)
    pad[1 : LX + 1, 8 : 8 + LY, :] = leaf

    load_basis.wait()
    grams = []
    for j in range(KB):
        for k in range(j, KB):
            grams.append(fold(basis[j] * basis[k]))
    gbuf[gx, 0:1, :] = to_lanes(grams)
    send_x(gbuf, g_sem, 1)

    load_bloch.wait()
    theta = (bloch[0], bloch[1])
    weights = far_weights(nx, ny, gx, gy, theta)
    far_w[0], far_w[1] = split(weights)

    load_type.wait()
    codes = boxes + BOXES * kind[...]
    for r in range(SD // COEF):
        code = jnp.broadcast_to(codes[r : r + 1, :], (COEF, COEF)).T
        own_box = code & (BOXES - 1)
        own_type = code >> 8
        lane = iota((COEF, COEF), 1)
        rows = pl.ds(r * COEF, COEF)
        member_t[rows, 0:COEF] = ones_where(own_box == lane)
        member_t[rows, COEF:BOXES] = ones_where(own_box == lane + COEF)
        spot = own_type * 8 + ((own_box >> 7) & 1) * 2 + ((own_box >> 3) & 1)
        hot[rows, :] = ones_where(spot == (lane & 63))
        field[rows, :] = own_type

    load_top.wait()
    load_tmats.wait()
    every = jnp.concatenate([tmats[t] for t in range(NTYPE)], axis=1)
    every_high, every_low = split(every)
    top_high, top_low = split(top[...])
    top_t[0], top_t[1] = split(dot(top_high, every_high) + dot(top_low, every_high) + dot(top_high, every_low))
    every3 = jnp.concatenate([every_high, every_high, every_low], axis=0)

    load_offsets.wait()
    load_near.wait()
    for copy in halo:
        copy.wait_recv()
    crossings = []
    row_cross = {-1: jnp.where(gx == 0, -1.0, 0.0), 0: 0.0, 1: jnp.where(gx == nx - 1, 1.0, 0.0)}
    col_cross = {-1: jnp.where(gy == 0, -1.0, 0.0), 0: 0.0, 1: jnp.where(gy == ny - 1, 1.0, 0.0)}
    angle = jnp.zeros((8, COEF), f32)
    for i, side in enumerate(sides):
        value = row_cross[side[0]] * theta[0] + col_cross[side[1]] * theta[1]
        angle = jnp.where(iota((8, COEF), 0) == i, value, angle)
    cosine, sine = jnp.cos(angle), jnp.sin(angle)

    def rotated(x, i):
        return cosine[i : i + 1] * x + sine[i : i + 1] * times_i(x)

    pad[0, 8 : 8 + LY, :] = rotated(rim[0], 0)
    pad[LX + 1, 8 : 8 + LY, :] = rotated(rim[1], 1)
    west, east = rotated(rim[2], 2), rotated(rim[3], 3)
    for x in range(LX):
        pad[x + 1, 7:8, :] = west[x : x + 1, :]
        pad[x + 1, 8 + LY : 9 + LY, :] = east[x : x + 1, :]
    for c, (x, y) in enumerate([(0, 7), (0, 8 + LY), (LX + 1, 7), (LX + 1, 8 + LY)]):
        pad[x, y : y + 1, :] = rotated(rim_corners[c], 4 + c)

    highs, lows, mats_high, mats_low = [], [], [], []
    for b in (-1, 0, 1):
        shifted = pad[:, 8 + b : 8 + b + LY, :].reshape((LX + 2) * LY, COEF)
        high, low = split(shifted)
        for a in (-1, 0, 1):
            entry = 0
            for o in range(NOFF):
                here = (offsets[o, 0] == a) & (offsets[o, 1] == b)
                entry = jnp.where(here, o, entry)
            mat_high, mat_low = split(near_mats[entry])
            start = (1 + a) * LY
            highs.append(high[start : start + BOXES])
            lows.append(low[start : start + BOXES])
            mats_high.append(mat_high)
            mats_low.append(mat_low)
    mat_high = jnp.concatenate(mats_high, axis=0)
    mats = jnp.concatenate([mat_high, jnp.concatenate(mats_low, axis=0)], axis=1)
    near2 = dot(jnp.concatenate(highs, axis=1), mats)
    near = near2[:, :COEF] + near2[:, COEF:] + dot(jnp.concatenate(lows, axis=1), mat_high)

    wait_all(ebuf, e_sem.at[1], nx - 1, 4)
    sources = ebuf[...].reshape(8 * nx, COEF)
    turned = pltpu.roll(times_i(sources), 4, 0)
    sources = jnp.where((iota(sources.shape, 0) & 4) == 0, sources, turned)
    source_high, source_low = split(sources)
    part2 = dot(far_w[0], jnp.concatenate([source_high, source_low], axis=1))
    part = part2[:, :COEF] + part2[:, COEF:] + dot(far_w[1], source_high)
    wait_all(gbuf, g_sem.at[1], nx - 1, 1)
    gram_column = jnp.sum(gbuf[...], axis=0)
    for j in range(ny):
        pbuf[j, 0:4, :] = part[4 * j : 4 * j + 4]
        pbuf[j, 4:5, :] = gram_column
    rbuf[gy, 0:5, :] = pbuf[gy, 0:5, :]
    send_y(pbuf, rbuf, r_sem, 5, True)

    near_pair = jnp.concatenate(split(near), axis=1)
    for r in range(SD // CHUNK):
        rows = pl.ds(r * CHUNK, CHUNK)
        at2 = dot(member_t[rows, :], near_pair)
        at_high, at_low = split(at2[:, :COEF] + at2[:, COEF:])
        all_types = dot(jnp.concatenate([at_high, at_low, at_high], axis=1), every3)
        own_type = field[rows, :]
        value = all_types[:, :COEF]
        for t in range(1, NTYPE):
            value = jnp.where(own_type == t, all_types[:, t * COEF : (t + 1) * COEF], value)
        image[rows, :] = basis[KB - 1, rows, :] - value

    wait_all(rbuf, r_sem.at[1], ny - 1, 5)
    arrived = jnp.sum(rbuf[...], axis=0)
    far = jnp.where(iota((8, COEF), 0) < 4, arrived, 0.0)
    gram_row = arrived[4:5, :]
    far_high, far_low = split(far)
    far_pair = jnp.concatenate([far_high.astype(f32), far_low.astype(f32)], axis=0).astype(bf16)
    table2 = dot(far_pair, top_t[0]) + dot(far_pair, top_t[1])
    table = table2[0:8] + table2[8:16]
    table = jnp.concatenate([table[:, t * COEF : (t + 1) * COEF] for t in range(NTYPE)], axis=0)
    table = jnp.concatenate(split(table), axis=0)

    gram, lane = {}, 0
    for j in range(KB):
        for k in range(j, KB):
            gram[j, k] = gram[k, j] = total_lane(gram_row, lane)
            lane += 1
    guess = [gram[k, KB - 1] / count for k in range(KB)]
    sums = [jnp.zeros((8, COEF), f32)] * (KB + 1)
    for r in range(SD // CHUNK):
        rows = pl.ds(r * CHUNK, CHUNK)
        w = image[rows, :] - dot(hot[rows, :], table)
        vectors = [basis[k, rows, :] for k in range(KB)]
        for k in range(KB):
            w = w - guess[k] * vectors[k]
        image[rows, :] = w
        for k in range(KB):
            sums[k] = sums[k] + fold(vectors[k] * w)
        sums[KB] = sums[KB] + fold(w * w)

    abuf[gx, 0:1, :] = to_lanes(sums)
    send_x(abuf, a_sem, 1)
    wait_all(abuf, a_sem.at[1], nx - 1, 1)
    bbuf[gy, 0:1, :] = jnp.sum(abuf[...], axis=0)
    send_y(bbuf, bbuf, b_sem, 1, False)
    wait_all(bbuf, b_sem.at[1], ny - 1, 1)
    totals = jnp.sum(bbuf[...], axis=0)
    inner = [total_lane(totals, k) for k in range(KB)]
    square = total_lane(totals, KB)
    coeffs = []
    for k in range(KB):
        value = inner[k]
        for j in range(KB):
            value = value + gram[k, j] * guess[j]
        coeffs.append(value / count)
    step = [coeffs[k] - guess[k] for k in range(KB)]
    for k in range(KB):
        along = -2.0 * inner[k]
        for j in range(KB):
            along = along + gram[k, j] * step[j]
        square = square + step[k] * along
    beta = jnp.sqrt(jnp.maximum(square, 0.0) / count + 1e-06)
    scale = 1.0 / beta

    outs = []
    for r in range(SD // CHUNK):
        rows = pl.ds(r * CHUNK, CHUNK)
        w = image[rows, :]
        for k in range(KB):
            w = w - step[k] * basis[k, rows, :]
        image[rows, :] = w * scale
        copy = pltpu.make_async_copy(image.at[rows], out_ref.at[rows], out_sem.at[r])
        copy.start()
        outs.append(copy)
    for k, value in enumerate(coeffs + [beta]):
        hess_ref[k] = jnp.sum(value)
    for copy in halo:
        copy.wait_send()
    wait_all(ebuf, e_sem.at[0], nx - 1, 4)
    wait_all(gbuf, g_sem.at[0], nx - 1, 1)
    wait_all(pbuf, r_sem.at[0], ny - 1, 5)
    wait_all(abuf, a_sem.at[0], nx - 1, 1)
    wait_all(bbuf, b_sem.at[0], ny - 1, 1)
    for copy in outs:
        copy.wait()


def on_device(nx, ny, basis, sphere_box, sphere_type, near_offsets, near_mats, up_mat, top_mat, tmats, bloch_angle):
    vmem, dma = pltpu.VMEM, pltpu.SemaphoreType.DMA
    return pl.pallas_call(
        functools.partial(kernel, nx, ny),
        out_shape=(jax.ShapeDtypeStruct((SD, COEF), f32), jax.ShapeDtypeStruct((KB + 1,), f32)),
        in_specs=[pl.BlockSpec(memory_space=pl.ANY)] * 9,
        out_specs=(pl.BlockSpec(memory_space=pl.ANY), pl.BlockSpec(memory_space=pltpu.SMEM)),
        scratch_shapes=[
            vmem((KB, SD, COEF), f32),
            vmem((SD // COEF, COEF), i32),
            vmem((SD // COEF, COEF), i32),
            pltpu.SMEM((NOFF, 2), i32),
            vmem((NOFF, COEF, COEF), f32),
            vmem((COEF, COEF), f32),
            vmem((COEF, COEF), f32),
            vmem((NTYPE, COEF, COEF), f32),
            pltpu.SMEM((2,), f32),
            vmem((nx, 8, COEF), f32),
            vmem((nx, 1, COEF), f32),
            vmem((ny, 8, COEF), f32),
            vmem((ny, 8, COEF), f32),
            vmem((nx, 1, COEF), f32),
            vmem((ny, 1, COEF), f32),
            vmem((4, LX, COEF), f32),
            vmem((4, 1, COEF), f32),
            vmem((4, LX, COEF), f32),
            vmem((4, 1, COEF), f32),
            vmem((LX + 2, LY + 16, COEF), f32),
            vmem((2, 4 * ny, 8 * nx), bf16),
            vmem((2, COEF, NTYPE * COEF), bf16),
            vmem((SD, COEF), bf16),
            vmem((SD, BOXES), bf16),
            vmem((SD, COEF), f32),
            vmem((SD, COEF), i32),
            dma((10,)),
            dma((2,)),
            dma((2,)),
            dma((2,)),
            dma((2,)),
            dma((2,)),
            dma((8,)),
            dma((8,)),
            dma((SD // CHUNK,)),
        ],
        compiler_params=pltpu.CompilerParams(
            collective_id=0, has_side_effects=True, vmem_limit_bytes=48 * 1024 * 1024
        ),
        name="arnoldi_step",
    )(
        basis,
        sphere_box.reshape(SD // COEF, COEF),
        sphere_type.reshape(SD // COEF, COEF),
        near_offsets, near_mats, up_mat, top_mat, tmats, bloch_angle,
    )


def solution(mesh):
    return jax.shard_map(
        functools.partial(on_device, mesh.shape["gx"], mesh.shape["gy"]),
        mesh=mesh,
        in_specs=(
            P(None, ("gx", "gy"), None),
            P(("gx", "gy")),
            P(("gx", "gy")),
            P(),
            P(),
            P(),
            P(),
            P(),
            P(),
        ),
        out_specs=(P(("gx", "gy"), None), P()),
        check_vma=False,
    )
```

time: 1010 us -> 58.8 us (0.06)
  waiting for transfers between devices: 716 us -> 0 us
  blocking collectives: 199 us -> 0 us
  Pallas kernels: 0 us -> 48.5 us
  matrix products: 28 us -> 0 us
  starting transfers between devices: 21.4 us -> 0 us
  between operations: 15 us -> 0.65 us
  local copies, waits for them, and re-layouts: 19.9 us -> 9.29 us
    all_gather x1 -> x0, waiting for transfers between devices: 714 us -> none  [on_device(): piece = lax.all_gather(expansion, ('gx', 'gy'), axis=0, tiled=True)]
    psum x2 -> x0, blocking collectives: 199 us -> none  [the longest x1 101 us: on_device(): coeffs = lax.psum(local_products, ('gx', 'gy')) / count]
    pallas_call x0 -> x1, Pallas kernels: none -> 48.5 us  [on_device(): pl.pallas_call(functools.partial(kernel, nx, ny), out_shape=(jax.ShapeDty...]
    dot_general x11 -> x0, matrix products: 28 us -> none  [the longest x8 18.5 us: product(): jnp.dot(left, right, precision=HIGHEST, preferred_element_type=jnp.float32)]
    ppermute x4 -> x0, starting transfers between devices: 21.3 us -> none  [the longest x2 13.9 us: extended(): after = lax.ppermute(leading, axis, down)]
    gather x27 -> x0, local copies, waits for them, and re-layouts: 17.2 us -> none
  transfers between devices with their start and end apart: 5 -> 0, of which waited for: 2 -> 0; matrix products, arithmetic and copies ran while one was open for 3% -> 0% of each run, Pallas kernels for 0% -> 0%
where the time goes in v1:
time: 58.8 us; the launch traced here: 58.4 us
  Pallas kernels  48.5 us (82%)
  local copies, waits for them, and re-layouts  9.29 us (16%)
  between operations  0.65 us (1%)
    pallas_call x1, Pallas kernels, on_device(): pl.pallas_call(functools.partial(kernel, nx, ny), out_shape=(jax.ShapeDty...  48.5 us
    unnamed x19, local copies, waits for them, and re-layouts  9.29 us

profile of v1, /device:TPU:1, one launch (start us, length us, event | category | flops | bytes accessed | tf_op | source)
XLA Modules:
  0.0 58.4 jit_solution(6729799964860081712)
XLA Ops:
  0.6 0.8 %copy.11.offsets_in = s32[9,2]{1,0:T(8,128)S(1)} copy(s32[9,2]{0,1:T(2,128)} %param.12) | data formatting | bytes 144 | tf_op args[3]
  1.4 0.0 copy-start
  1.4 1.4 %copy-done = f32[3,1024,128]{2,1,0:T(8,128)S(1)} copy-done((f32[3,1024,128]{2,1,0:T(8,128)S(1)}, f32[3,1024,128]{2,1,0:T(8,128)}, u32[]{:S(2)}) %copy-start) | copy-done | bytes 1572888
  2.8 0.0 copy-start.1
  2.8 1.1 %copy-done.1 = f32[9,128,128]{2,1,0:T(8,128)S(1)} copy-done((f32[9,128,128]{2,1,0:T(8,128)S(1)}, f32[9,128,128]{2,1,0:T(8,128)}, u32[]{:S(2)}) %copy-start.1) | copy-done | bytes 589848
  3.9 0.0 copy-start.2
  3.9 1.0 %copy-done.2 = f32[8,128,128]{2,1,0:T(8,128)S(1)} copy-done((f32[8,128,128]{2,1,0:T(8,128)S(1)}, f32[8,128,128]{2,1,0:T(8,128)}, u32[]{:S(2)}) %copy-start.2) | copy-done | bytes 524312
  4.9 0.0 copy-start.3
  4.9 0.8 %copy-done.3 = f32[128,128]{1,0:T(8,128)S(1)} copy-done((f32[128,128]{1,0:T(8,128)S(1)}, f32[128,128]{1,0:T(8,128)}, u32[]{:S(2)}) %copy-start.3) | copy-done | bytes 65560
  5.8 0.0 copy-start.4
  5.8 0.8 %copy-done.4 = f32[128,128]{1,0:T(8,128)S(1)} copy-done((f32[128,128]{1,0:T(8,128)S(1)}, f32[128,128]{1,0:T(8,128)}, u32[]{:S(2)}) %copy-start.4) | copy-done | bytes 65560
  6.6 0.0 copy-start.5
  6.6 0.7 %copy-done.5 = s32[1024]{0:T(1024)S(1)} copy-done((s32[1024]{0:T(1024)S(1)}, s32[1024]{0:T(1024)}, u32[]{:S(2)}) %copy-start.5) | copy-done | bytes 4120
  7.3 0.0 copy-start.6
  7.3 0.7 %copy-done.6 = s32[1024]{0:T(1024)S(1)} copy-done((s32[1024]{0:T(1024)S(1)}, s32[1024]{0:T(1024)}, u32[]{:S(2)}) %copy-start.6) | copy-done | bytes 4120
  8.0 0.0 copy-start.7
  8.0 0.7 %copy-done.7 = f32[2]{0:T(128)S(1)} copy-done((f32[2]{0:T(128)S(1)}, f32[2]{0:T(128)}, u32[]{:S(2)}) %copy-start.7) | copy-done | bytes 32
  8.6 48.5 %arnoldi_step.1 = (f32[1024,128]{1,0:T(8,128)S(1)}, f32[4]{0:T(128)S(1)}) custom-call(f32[3,1024,128]{2,1,0:T(8,128)S(1)} %copy-done, s32[8,128]{1,0:T(8,128)S(1)} %bitcast.2, s32[8,128]{1,0:T(8,128)S(1)} %bitcast.3, s32[9,2]{1,0:T(8,128)S(1)} %copy.11.offsets_in, f32[9,128,128]{2,1,0:T(8,128)S(1)} %copy-done.1, f32[128,128]{1,0:T(8,128)S(1)} %copy-done.3, ...), custom_call_target="tpu_custom_call" | custom-call | tf_op jit(solution)/shard_map/arnoldi_step/pallas_call | solution.py:389
  57.1 0.8 %copy.14 = f32[1024,128]{1,0:T(8,128)} copy(f32[1024,128]{1,0:T(8,128)S(1)} %get-tuple-element.4) | data formatting | bytes 1048576
  57.9 0.5 copy.15
Async XLA Ops:
  1.4 1.4 %copy-start = (f32[3,1024,128]{2,1,0:T(8,128)S(1)}, f32[3,1024,128]{2,1,0:T(8,128)}, u32[]{:S(2)}) copy-start(f32[3,1024,128]{2,1,0:T(8,128)} %basis_in.1) | copy-start | bytes 4718596
  2.8 1.1 %copy-start.1 = (f32[9,128,128]{2,1,0:T(8,128)S(1)}, f32[9,128,128]{2,1,0:T(8,128)}, u32[]{:S(2)}) copy-start(f32[9,128,128]{2,1,0:T(8,128)} %near_in.1) | copy-start | bytes 1769476
  3.9 1.0 %copy-start.2 = (f32[8,128,128]{2,1,0:T(8,128)S(1)}, f32[8,128,128]{2,1,0:T(8,128)}, u32[]{:S(2)}) copy-start(f32[8,128,128]{2,1,0:T(8,128)} %tmats_in.1) | copy-start | bytes 1572868
  4.9 0.8 %copy-start.3 = (f32[128,128]{1,0:T(8,128)S(1)}, f32[128,128]{1,0:T(8,128)}, u32[]{:S(2)}) copy-start(f32[128,128]{1,0:T(8,128)} %up_in.1) | copy-start | bytes 196612
  5.8 0.8 %copy-start.4 = (f32[128,128]{1,0:T(8,128)S(1)}, f32[128,128]{1,0:T(8,128)}, u32[]{:S(2)}) copy-start(f32[128,128]{1,0:T(8,128)} %top_in.1) | copy-start | bytes 196612
  6.6 0.7 %copy-start.5 = (s32[1024]{0:T(1024)S(1)}, s32[1024]{0:T(1024)}, u32[]{:S(2)}) copy-start(s32[1024]{0:T(1024)} %param.10) | copy-start | bytes 12292
  7.3 0.7 %copy-start.6 = (s32[1024]{0:T(1024)S(1)}, s32[1024]{0:T(1024)}, u32[]{:S(2)}) copy-start(s32[1024]{0:T(1024)} %param.11) | copy-start | bytes 12292
  8.0 0.7 %copy-start.7 = (f32[2]{0:T(128)S(1)}, f32[2]{0:T(128)}, u32[]{:S(2)}) copy-start(f32[2]{0:T(128)} %bloch_in.1) | copy-start | bytes 28

commit v2 on v1

--- a/solution.py
+++ b/solution.py
@@ -16,6 +16,7 @@
 NOFF = 9
 BOXES = LX * LY
 CHUNK = 256
+SAMPLE = 128
 
 MESH = pl.DeviceIdType.MESH
 wave_number = 2.3
@@ -51,10 +52,11 @@
 
 
 def to_lanes(parts):
+    size = -(-len(parts) // 8) * 8
     rows = [jnp.sum(p, axis=0, keepdims=True) for p in parts]
-    rows += [jnp.zeros((8 - len(rows), COEF), f32)]
+    rows += [jnp.zeros((size - len(rows), COEF), f32)]
     sums = jnp.sum(jnp.concatenate(rows, axis=0), axis=1, keepdims=True)
-    placed = jnp.where(iota((8, COEF), 0) == iota((8, COEF), 1), sums, 0.0)
+    placed = jnp.where(iota((size, COEF), 0) == iota((size, COEF), 1), sums, 0.0)
     return jnp.sum(placed, axis=0, keepdims=True)
 
 
@@ -62,12 +64,14 @@
     return jnp.sum(x.reshape(x.shape[0] // 8, 8, COEF), axis=0)
 
 
-def far_weights(nx, ny, gx, gy, theta):
-    shape = (4 * ny, 8 * nx)
+def far_weights(nx, ny, nz, gx, gy, theta):
+    shape = (8 * ny, 8 * nz)
     m, n = iota(shape, 0), iota(shape, 1)
     grid_x, grid_y = 2 * nx, 2 * ny
-    target_x, target_y = 2 * gx + ((m >> 1) & 1), 2 * (m >> 2) + (m & 1)
-    source_x, source_y = 2 * (n >> 3) + ((n >> 1) & 1), 2 * gy + (n & 1)
+    target_row = jnp.where(m >= 4 * ny, nz, 0) + gx % nz
+    target_x, target_y = 2 * target_row + ((m >> 1) & 1), 2 * ((m >> 2) & (ny - 1)) + (m & 1)
+    source_row = (gx // nz) * nz + (n >> 3)
+    source_x, source_y = 2 * source_row + ((n >> 1) & 1), 2 * gy + (n & 1)
     shift_x = ((source_x - target_x + grid_x // 2) & (grid_x - 1)) - grid_x // 2
     shift_y = ((source_y - target_y + grid_y // 2) & (grid_y - 1)) - grid_y // 2
     wraps_x, wraps_y = target_x + shift_x - source_x, target_y + shift_y - source_y
@@ -86,11 +90,15 @@
     basis_in, box_in, type_in, offsets_in, near_in, up_in, top_in, tmats_in, bloch_in,
     out_ref, hess_ref,
     basis, box, kind, offsets, near_mats, up, top, tmats, bloch,
-    ebuf, gbuf, pbuf, rbuf, abuf, bbuf,
+    ebuf, pbuf, rbuf, abuf, bbuf,
     edges, corners, rim, rim_corners, pad, far_w, top_t, hot, member_t, image, field,
-    load_sem, e_sem, g_sem, r_sem, a_sem, b_sem, h_send, h_recv, out_sem,
+    load_sem, e_sem, r_sem, a_sem, b_sem, h_send, h_recv, out_sem,
 ):
     gx, gy = lax.axis_index("gx"), lax.axis_index("gy")
+    nz = nx // 2
+    planes = 2 * ny
+    half, z = gx // nz, gx % nz
+    spot_in_plane = half * ny + gy
     count = float(nx * ny * SD * COEF)
 
     def load(src, dst, i):
@@ -102,56 +110,69 @@
     load_box = load(box_in, box, 1)
     load_up = load(up_in, up, 2)
     load_bloch = load(bloch_in, bloch, 3)
-    load_basis = load(basis_in.at[pl.ds(0, KB - 1)], basis.at[pl.ds(0, KB - 1)], 4)
+    others = pl.ds(0, KB - 1)
+    load_sample = load(basis_in.at[others, pl.ds(0, SAMPLE)], basis.at[others, pl.ds(0, SAMPLE)], 4)
     load_type = load(type_in, kind, 5)
     load_offsets = load(offsets_in, offsets, 6)
     load_near = load(near_in, near_mats, 7)
     load_top = load(top_in, top, 8)
     load_tmats = load(tmats_in, tmats, 9)
+    rest = pl.ds(SAMPLE, SD - SAMPLE)
+    load_basis = load(basis_in.at[others, rest], basis.at[others, rest], 10)
 
     barrier = pltpu.get_barrier_semaphore()
 
-    def greet_x(k, c):
-        pl.semaphore_signal(barrier, inc=1, device_id={"gx": (gx + k) % nx}, device_id_type=MESH)
+    def in_line(k):
+        return {"gx": half * nz + (z + k) % nz}
+
+    def in_plane(k):
+        peer = (spot_in_plane + k) % planes
+        return peer, {"gx": (peer // ny) * nz + z, "gy": peer % ny}
+
+    def greet_line(k, c):
+        pl.semaphore_signal(barrier, inc=1, device_id=in_line(k), device_id_type=MESH)
         return c
 
-    def greet_y(k, c):
-        pl.semaphore_signal(barrier, inc=1, device_id={"gy": (gy + k) % ny}, device_id_type=MESH)
+    def greet_plane(k, c):
+        pl.semaphore_signal(barrier, inc=1, device_id=in_plane(k)[1], device_id_type=MESH)
         return c
 
-    lax.fori_loop(1, nx, greet_x, 0)
-    lax.fori_loop(1, ny, greet_y, 0)
+    lax.fori_loop(1, nz, greet_line, 0)
+    lax.fori_loop(1, planes, greet_plane, 0)
     sides = [(-1, 0), (1, 0), (0, -1), (0, 1), (-1, -1), (-1, 1), (1, -1), (1, 1)]
 
     def beside(side):
         return {"gx": (gx + side[0] + nx) % nx, "gy": (gy + side[1] + ny) % ny}
 
-    for side in sides[4:]:
+    for side in sides:
         pl.semaphore_signal(barrier, inc=1, device_id=beside(side), device_id_type=MESH)
 
-    def send_x(buf, sem, rows):
+    pending = []
+
+    def send_line(buf, sem, rows):
         def body(k, c):
-            near_half = nx // 2 + ((k + 1) // 2) * (1 - 2 * (k % 2))
-            peer = (gx + near_half) % nx
-            spot = buf.at[gx, pl.ds(0, rows)]
+            far_half = nz // 2 + ((k + 1) // 2) * (1 - 2 * (k % 2))
+            spot = buf.at[z, pl.ds(0, rows)]
             pltpu.make_async_remote_copy(
-                spot, spot, sem.at[0], sem.at[1], device_id={"gx": peer}, device_id_type=MESH
+                spot, spot, sem.at[0], sem.at[1], device_id=in_line(far_half), device_id_type=MESH
             ).start()
             return c
 
-        lax.fori_loop(0, nx - 1, body, 0)
-
-    def send_y(src, dst, sem, rows, scatter):
+        lax.fori_loop(0, nz - 1, body, 0)
+        pending.append((buf, sem, nz - 1, rows))
+
+    def send_plane(src, dst, sem, rows, scatter):
         def body(k, c):
-            peer = (gy + k) % ny
+            peer, device = in_plane(k)
             pltpu.make_async_remote_copy(
-                src.at[peer if scatter else gy, pl.ds(0, rows)],
-                dst.at[gy, pl.ds(0, rows)],
-                sem.at[0], sem.at[1], device_id={"gy": peer}, device_id_type=MESH,
+                src.at[peer if scatter else spot_in_plane, pl.ds(0, rows)],
+                dst.at[spot_in_plane, pl.ds(0, rows)],
+                sem.at[0], sem.at[1], device_id=device, device_id_type=MESH,
             ).start()
             return c
 
-        lax.fori_loop(1, ny, body, 0)
+        lax.fori_loop(1, planes, body, 0)
+        pending.append((src, sem, planes - 1, rows))
 
     def wait_all(buf, sem, number, rows):
         span = buf.at[pl.ds(0, number), pl.ds(0, rows)]
@@ -159,27 +180,30 @@
 
     load_box.wait()
     boxes = box[...]
+    quarters = ((boxes >> 7) & 1) * 2 + ((boxes >> 3) & 1)
+    quarter_of = jnp.concatenate(
+        [ones_where(iota((16, COEF), 0) == quarters[r : r + 1, :]) for r in range(SD // COEF)], axis=1
+    )
+    load_up.wait()
+    up_high, up_low = split(up[...])
+    load_vec.wait()
+    vector_pair = jnp.concatenate(split(basis[KB - 1]), axis=1)
+    quad2 = dot(quarter_of, vector_pair)
+    quad_high, quad_low = split((quad2[:, :COEF] + quad2[:, COEF:])[0:8])
+    pair = jnp.concatenate([quad_high.astype(f32), quad_low.astype(f32)], axis=0).astype(bf16)
+    raised = dot(pair, up_high) + dot(pair, up_low)
+    ebuf[z, 0:4, :] = (raised[0:8] + raised[8:16])[0:4]
+    load_sample.wait()
+    sampled = [basis[k, 0:SAMPLE, :] for k in range(KB)]
+    ebuf[z, 4:5, :] = to_lanes([fold(v * sampled[KB - 1]) for v in sampled])
+    pl.semaphore_wait(barrier, nz + planes + 6)
+    send_line(ebuf, e_sem, 5)
+
     member = jnp.concatenate(
         [ones_where(iota((BOXES, COEF), 0) == boxes[r : r + 1, :]) for r in range(SD // COEF)], axis=1
     )
-    load_vec.wait()
-    leaf2 = dot(member, jnp.concatenate(split(basis[KB - 1]), axis=1))
+    leaf2 = dot(member, vector_pair)
     leaf = (leaf2[:, :COEF] + leaf2[:, COEF:]).reshape(LX, LY, COEF)
-
-    quads = []
-    for a in range(2):
-        for b in range(2):
-            part = jnp.sum(leaf[a * 8 : a * 8 + 8, b * 8 : b * 8 + 8, :], axis=0)
-            quads.append(jnp.sum(part, axis=0, keepdims=True))
-    quad_sum = jnp.concatenate(quads + [jnp.zeros((4, COEF), f32)], axis=0)
-    load_up.wait()
-    quad_high, quad_low = split(quad_sum)
-    pair = jnp.concatenate([quad_high.astype(f32), quad_low.astype(f32)], axis=0).astype(bf16)
-    up_high, up_low = split(up[...])
-    raised = dot(pair, up_high) + dot(pair, up_low)
-    ebuf[gx, 0:4, :] = (raised[0:8] + raised[8:16])[0:4]
-    pl.semaphore_wait(barrier, nx + ny + 2)
-    send_x(ebuf, e_sem, 4)
 
     edges[0] = leaf[0]
     edges[1] = leaf[LX - 1]
@@ -206,12 +230,10 @@
     for j in range(KB):
         for k in range(j, KB):
             grams.append(fold(basis[j] * basis[k]))
-    gbuf[gx, 0:1, :] = to_lanes(grams)
-    send_x(gbuf, g_sem, 1)
 
     load_bloch.wait()
     theta = (bloch[0], bloch[1])
-    weights = far_weights(nx, ny, gx, gy, theta)
+    weights = far_weights(nx, ny, nz, gx, gy, theta)
     far_w[0], far_w[1] = split(weights)
 
     load_type.wait()
@@ -268,7 +290,7 @@
         for a in (-1, 0, 1):
             entry = 0
             for o in range(NOFF):
-                here = (offsets[o, 0] == a) & (offsets[o, 1] == b)
+                here = (offsets[0, o] == a) & (offsets[1, o] == b)
                 entry = jnp.where(here, o, entry)
             mat_high, mat_low = split(near_mats[entry])
             start = (1 + a) * LY
@@ -281,20 +303,20 @@
     near2 = dot(jnp.concatenate(highs, axis=1), mats)
     near = near2[:, :COEF] + near2[:, COEF:] + dot(jnp.concatenate(lows, axis=1), mat_high)
 
-    wait_all(ebuf, e_sem.at[1], nx - 1, 4)
-    sources = ebuf[...].reshape(8 * nx, COEF)
+    wait_all(ebuf, e_sem.at[1], nz - 1, 5)
+    blocks = ebuf[...]
+    sources = blocks.reshape(8 * nz, COEF)
     turned = pltpu.roll(times_i(sources), 4, 0)
     sources = jnp.where((iota(sources.shape, 0) & 4) == 0, sources, turned)
     source_high, source_low = split(sources)
     part2 = dot(far_w[0], jnp.concatenate([source_high, source_low], axis=1))
     part = part2[:, :COEF] + part2[:, COEF:] + dot(far_w[1], source_high)
-    wait_all(gbuf, g_sem.at[1], nx - 1, 1)
-    gram_column = jnp.sum(gbuf[...], axis=0)
-    for j in range(ny):
+    sample_sum = jnp.sum(blocks, axis=0)[4:5, :]
+    for j in range(planes):
         pbuf[j, 0:4, :] = part[4 * j : 4 * j + 4]
-        pbuf[j, 4:5, :] = gram_column
-    rbuf[gy, 0:5, :] = pbuf[gy, 0:5, :]
-    send_y(pbuf, rbuf, r_sem, 5, True)
+        pbuf[j, 4:5, :] = sample_sum
+    rbuf[spot_in_plane, 0:5, :] = pbuf[spot_in_plane, 0:5, :]
+    send_plane(pbuf, rbuf, r_sem, 5, True)
 
     near_pair = jnp.concatenate(split(near), axis=1)
     for r in range(SD // CHUNK):
@@ -308,10 +330,10 @@
             value = jnp.where(own_type == t, all_types[:, t * COEF : (t + 1) * COEF], value)
         image[rows, :] = basis[KB - 1, rows, :] - value
 
-    wait_all(rbuf, r_sem.at[1], ny - 1, 5)
+    wait_all(rbuf, r_sem.at[1], planes - 1, 5)
     arrived = jnp.sum(rbuf[...], axis=0)
     far = jnp.where(iota((8, COEF), 0) < 4, arrived, 0.0)
-    gram_row = arrived[4:5, :]
+    sample_row = arrived[4:5, :]
     far_high, far_low = split(far)
     far_pair = jnp.concatenate([far_high.astype(f32), far_low.astype(f32)], axis=0).astype(bf16)
     table2 = dot(far_pair, top_t[0]) + dot(far_pair, top_t[1])
@@ -319,12 +341,8 @@
     table = jnp.concatenate([table[:, t * COEF : (t + 1) * COEF] for t in range(NTYPE)], axis=0)
     table = jnp.concatenate(split(table), axis=0)
 
-    gram, lane = {}, 0
-    for j in range(KB):
-        for k in range(j, KB):
-            gram[j, k] = gram[k, j] = total_lane(gram_row, lane)
-            lane += 1
-    guess = [gram[k, KB - 1] / count for k in range(KB)]
+    sample_count = float(nx * ny * SAMPLE * COEF)
+    guess = [total_lane(sample_row, k) / sample_count for k in range(KB)]
     sums = [jnp.zeros((8, COEF), f32)] * (KB + 1)
     for r in range(SD // CHUNK):
         rows = pl.ds(r * CHUNK, CHUNK)
@@ -337,15 +355,20 @@
             sums[k] = sums[k] + fold(vectors[k] * w)
         sums[KB] = sums[KB] + fold(w * w)
 
-    abuf[gx, 0:1, :] = to_lanes(sums)
-    send_x(abuf, a_sem, 1)
-    wait_all(abuf, a_sem.at[1], nx - 1, 1)
-    bbuf[gy, 0:1, :] = jnp.sum(abuf[...], axis=0)
-    send_y(bbuf, bbuf, b_sem, 1, False)
-    wait_all(bbuf, b_sem.at[1], ny - 1, 1)
+    abuf[z, 0:1, :] = to_lanes(sums + grams)
+    send_line(abuf, a_sem, 1)
+    wait_all(abuf, a_sem.at[1], nz - 1, 1)
+    bbuf[spot_in_plane, 0:1, :] = jnp.sum(abuf[...], axis=0)
+    send_plane(bbuf, bbuf, b_sem, 1, False)
+    wait_all(bbuf, b_sem.at[1], planes - 1, 1)
     totals = jnp.sum(bbuf[...], axis=0)
     inner = [total_lane(totals, k) for k in range(KB)]
     square = total_lane(totals, KB)
+    gram, lane = {}, KB + 1
+    for j in range(KB):
+        for k in range(j, KB):
+            gram[j, k] = gram[k, j] = total_lane(totals, lane)
+            lane += 1
     coeffs = []
     for k in range(KB):
         value = inner[k]
@@ -375,51 +398,47 @@
         hess_ref[k] = jnp.sum(value)
     for copy in halo:
         copy.wait_send()
-    wait_all(ebuf, e_sem.at[0], nx - 1, 4)
-    wait_all(gbuf, g_sem.at[0], nx - 1, 1)
-    wait_all(pbuf, r_sem.at[0], ny - 1, 5)
-    wait_all(abuf, a_sem.at[0], nx - 1, 1)
-    wait_all(bbuf, b_sem.at[0], ny - 1, 1)
+    for buf, sem, number, rows in pending:
+        wait_all(buf, sem.at[0], number, rows)
     for copy in outs:
         copy.wait()
 
 
 def on_device(nx, ny, basis, sphere_box, sphere_type, near_offsets, near_mats, up_mat, top_mat, tmats, bloch_angle):
+    nz = nx // 2
     vmem, dma = pltpu.VMEM, pltpu.SemaphoreType.DMA
     return pl.pallas_call(
         functools.partial(kernel, nx, ny),
         out_shape=(jax.ShapeDtypeStruct((SD, COEF), f32), jax.ShapeDtypeStruct((KB + 1,), f32)),
-        in_specs=[pl.BlockSpec(memory_space=pl.ANY)] * 9,
-        out_specs=(pl.BlockSpec(memory_space=pl.ANY), pl.BlockSpec(memory_space=pltpu.SMEM)),
+        in_specs=[pl.BlockSpec(memory_space=pltpu.HBM)] * 9,
+        out_specs=(pl.BlockSpec(memory_space=pltpu.HBM), pl.BlockSpec(memory_space=pltpu.SMEM)),
         scratch_shapes=[
             vmem((KB, SD, COEF), f32),
             vmem((SD // COEF, COEF), i32),
             vmem((SD // COEF, COEF), i32),
-            pltpu.SMEM((NOFF, 2), i32),
+            pltpu.SMEM((2, NOFF), i32),
             vmem((NOFF, COEF, COEF), f32),
             vmem((COEF, COEF), f32),
             vmem((COEF, COEF), f32),
             vmem((NTYPE, COEF, COEF), f32),
             pltpu.SMEM((2,), f32),
-            vmem((nx, 8, COEF), f32),
-            vmem((nx, 1, COEF), f32),
-            vmem((ny, 8, COEF), f32),
-            vmem((ny, 8, COEF), f32),
-            vmem((nx, 1, COEF), f32),
-            vmem((ny, 1, COEF), f32),
+            vmem((nz, 8, COEF), f32),
+            vmem((2 * ny, 8, COEF), f32),
+            vmem((2 * ny, 8, COEF), f32),
+            vmem((nz, 1, COEF), f32),
+            vmem((2 * ny, 1, COEF), f32),
             vmem((4, LX, COEF), f32),
             vmem((4, 1, COEF), f32),
             vmem((4, LX, COEF), f32),
             vmem((4, 1, COEF), f32),
             vmem((LX + 2, LY + 16, COEF), f32),
-            vmem((2, 4 * ny, 8 * nx), bf16),
+            vmem((2, 8 * ny, 8 * nz), bf16),
             vmem((2, COEF, NTYPE * COEF), bf16),
             vmem((SD, COEF), bf16),
             vmem((SD, BOXES), bf16),
             vmem((SD, COEF), f32),
             vmem((SD, COEF), i32),
-            dma((10,)),
-            dma((2,)),
+            dma((11,)),
             dma((2,)),
             dma((2,)),
             dma((2,)),
@@ -429,14 +448,14 @@
             dma((SD // CHUNK,)),
         ],
         compiler_params=pltpu.CompilerParams(
-            collective_id=0, has_side_effects=True, vmem_limit_bytes=48 * 1024 * 1024
+            collective_id=0, has_side_effects=True, vmem_limit_bytes=64 * 1024 * 1024
         ),
         name="arnoldi_step",
     )(
         basis,
         sphere_box.reshape(SD // COEF, COEF),
         sphere_type.reshape(SD // COEF, COEF),
-        near_offsets, near_mats, up_mat, top_mat, tmats, bloch_angle,
+        near_offsets.T, near_mats, up_mat, top_mat, tmats, bloch_angle,
     )
 
 

time: 58.8 us -> 47.5 us (0.81)
  local copies, waits for them, and re-layouts: 9.29 us -> 2.97 us
  Pallas kernels: 48.5 us -> 43.7 us
    unnamed x19 -> x2, local copies, waits for them, and re-layouts: 9.29 us -> 2.97 us
    pallas_call x1, Pallas kernels: 48.5 us -> 43.7 us  [on_device(): pl.pallas_call(functools.partial(kernel, nx, ny), out_shape=(jax.ShapeDty...]
where the time goes in v2:
time: 47.5 us; the launch traced here: 47.3 us
  Pallas kernels  43.7 us (92%)
  local copies, waits for them, and re-layouts  2.97 us (6%)
  between operations  0.64 us (1%)
    pallas_call x1, Pallas kernels, on_device(): pl.pallas_call(functools.partial(kernel, nx, ny), out_shape=(jax.ShapeDty...  43.7 us
    unnamed x2, local copies, waits for them, and re-layouts  2.97 us

profile of v2, /device:TPU:1, one launch (start us, length us, event | category | flops | bytes accessed | tf_op | source)
XLA Modules:
  0.0 47.3 jit_solution(1165371019115281665)
XLA Ops:
  0.6 43.7 %arnoldi_step.1 = (f32[1024,128]{1,0:T(8,128)}, f32[4]{0:T(128)}) custom-call(f32[3,1024,128]{2,1,0:T(8,128)} %basis_in.1, s32[8,128]{1,0:T(8,128)} %bitcast.3, s32[8,128]{1,0:T(8,128)} %bitcast.4, s32[2,9]{1,0:T(2,128)} %bitcast.5, f32[9,128,128]{2,1,0:T(8,128)} %near_in.1, f32[128,128]{1,0:T(8,128)} %up_in.1, f32[128,128]{1,0:T(8,128)} %top_in.1, ...), custom_call_target="tpu_custom_call" | custom-call | tf_op jit(solution)/shard_map/arnoldi_step/pallas_call | solution.py:410
  44.4 1.9 %copy.13 = f32[1024,128]{1,0:T(8,128)} copy(f32[1024,128]{1,0:T(8,128)} %get-tuple-element.4) | data formatting | bytes 1048576
  46.2 1.1 %copy.14 = f32[4]{0:T(128)} copy(f32[4]{0:T(128)} %get-tuple-element.5) | data formatting | bytes 32

commit v3 on v2

--- a/solution.py
+++ b/solution.py
@@ -390,10 +390,7 @@
         w = image[rows, :]
         for k in range(KB):
             w = w - step[k] * basis[k, rows, :]
-        image[rows, :] = w * scale
-        copy = pltpu.make_async_copy(image.at[rows], out_ref.at[rows], out_sem.at[r])
-        copy.start()
-        outs.append(copy)
+        out_ref[rows, :] = w * scale
     for k, value in enumerate(coeffs + [beta]):
         hess_ref[k] = jnp.sum(value)
     for copy in halo:
@@ -409,9 +406,9 @@
     vmem, dma = pltpu.VMEM, pltpu.SemaphoreType.DMA
     return pl.pallas_call(
         functools.partial(kernel, nx, ny),
-        out_shape=(jax.ShapeDtypeStruct((SD, COEF), f32), jax.ShapeDtypeStruct((KB + 1,), f32)),
+        out_shape=(pltpu.VMEM((SD, COEF), f32), pltpu.SMEM((KB + 1,), f32)),
         in_specs=[pl.BlockSpec(memory_space=pltpu.HBM)] * 9,
-        out_specs=(pl.BlockSpec(memory_space=pltpu.HBM), pl.BlockSpec(memory_space=pltpu.SMEM)),
+        out_specs=(pl.BlockSpec(memory_space=pltpu.VMEM), pl.BlockSpec(memory_space=pltpu.SMEM)),
         scratch_shapes=[
             vmem((KB, SD, COEF), f32),
             vmem((SD // COEF, COEF), i32),
@@ -448,14 +445,14 @@
             dma((SD // CHUNK,)),
         ],
         compiler_params=pltpu.CompilerParams(
-            collective_id=0, has_side_effects=True, vmem_limit_bytes=64 * 1024 * 1024
+            collective_id=0, has_side_effects=True, vmem_limit_bytes=48 * 1024 * 1024
         ),
         name="arnoldi_step",
     )(
-        basis,
+        *[pltpu.with_memory_space_constraint(x, pltpu.HBM) for x in (basis,
         sphere_box.reshape(SD // COEF, COEF),
         sphere_type.reshape(SD // COEF, COEF),
-        near_offsets.T, near_mats, up_mat, top_mat, tmats, bloch_angle,
+        near_offsets.T, near_mats, up_mat, top_mat, tmats, bloch_angle)]
     )
 
 

time: 47.5 us -> 44.6 us (0.939)
  local copies, waits for them, and re-layouts: 2.97 us -> 1.31 us
  Pallas kernels: 43.7 us -> 42.6 us
    unnamed x2, local copies, waits for them, and re-layouts: 2.97 us -> 1.31 us
    pallas_call x1, Pallas kernels: 43.7 us -> 42.6 us  [on_device(): pl.pallas_call(functools.partial(kernel, nx, ny), out_shape=(pltpu.VMEM((...]
where the time goes in v3:
time: 44.6 us; the launch traced here: 44.5 us
  Pallas kernels  42.6 us (96%)
  local copies, waits for them, and re-layouts  1.31 us (3%)
  between operations  0.64 us (1%)
    pallas_call x1, Pallas kernels, on_device(): pl.pallas_call(functools.partial(kernel, nx, ny), out_shape=(pltpu.VMEM((...  42.6 us
    unnamed x2, local copies, waits for them, and re-layouts  1.31 us

profile of v3, /device:TPU:1, one launch (start us, length us, event | category | flops | bytes accessed | tf_op | source)
XLA Modules:
  0.0 44.5 jit_solution(2719672120373947295)
XLA Ops:
  0.6 42.6 %arnoldi_step.1 = (f32[1024,128]{1,0:T(8,128)S(1)}, f32[4]{0:T(128)S(4)}) custom-call(f32[3,1024,128]{2,1,0:T(8,128)} %basis_in.1, s32[8,128]{1,0:T(8,128)} %bitcast.3, s32[8,128]{1,0:T(8,128)} %bitcast.4, s32[2,9]{1,0:T(2,128)} %bitcast.5, f32[9,128,128]{2,1,0:T(8,128)} %near_in.1, f32[128,128]{1,0:T(8,128)} %up_in.1, f32[128,128]{1,0:T(8,128)} %top_in.1, ...), custom_call_target="tpu_custom_call" | custom-call | tf_op jit(solution)/shard_map/arnoldi_step/pallas_call | solution.py:407
  43.2 0.8 %copy.13 = f32[1024,128]{1,0:T(8,128)} copy(f32[1024,128]{1,0:T(8,128)S(1)} %get-tuple-element.2) | data formatting | bytes 1048576
  44.0 0.5 %copy.14 = f32[4]{0:T(128)} copy(f32[4]{0:T(128)S(4)} %get-tuple-element.3) | data formatting | bytes 32

commit v4 on v3

--- a/solution.py
+++ b/solution.py
@@ -65,13 +65,13 @@
 
 
 def far_weights(nx, ny, nz, gx, gy, theta):
-    shape = (8 * ny, 8 * nz)
+    shape = (4 * nz, 16 * ny)
     m, n = iota(shape, 0), iota(shape, 1)
     grid_x, grid_y = 2 * nx, 2 * ny
-    target_row = jnp.where(m >= 4 * ny, nz, 0) + gx % nz
-    target_x, target_y = 2 * target_row + ((m >> 1) & 1), 2 * ((m >> 2) & (ny - 1)) + (m & 1)
-    source_row = (gx // nz) * nz + (n >> 3)
-    source_x, source_y = 2 * source_row + ((n >> 1) & 1), 2 * gy + (n & 1)
+    target_row = (gx // nz) * nz + (m >> 2)
+    target_x, target_y = 2 * target_row + ((m >> 1) & 1), 2 * gy + (m & 1)
+    source_row = jnp.where(n >= 8 * ny, nz, 0) + gx % nz
+    source_x, source_y = 2 * source_row + ((n >> 1) & 1), 2 * ((n >> 3) & (ny - 1)) + (n & 1)
     shift_x = ((source_x - target_x + grid_x // 2) & (grid_x - 1)) - grid_x // 2
     shift_y = ((source_y - target_y + grid_y // 2) & (grid_y - 1)) - grid_y // 2
     wraps_x, wraps_y = target_x + shift_x - source_x, target_y + shift_y - source_y
@@ -92,7 +92,7 @@
     basis, box, kind, offsets, near_mats, up, top, tmats, bloch,
     ebuf, pbuf, rbuf, abuf, bbuf,
     edges, corners, rim, rim_corners, pad, far_w, top_t, hot, member_t, image, field,
-    load_sem, e_sem, r_sem, a_sem, b_sem, h_send, h_recv, out_sem,
+    load_sem, e_sem, r_sem, a_sem, b_sem, h_send, h_recv, met,
 ):
     gx, gy = lax.axis_index("gx"), lax.axis_index("gy")
     nz = nx // 2
@@ -129,37 +129,38 @@
         peer = (spot_in_plane + k) % planes
         return peer, {"gx": (peer // ny) * nz + z, "gy": peer % ny}
 
-    def greet_line(k, c):
-        pl.semaphore_signal(barrier, inc=1, device_id=in_line(k), device_id_type=MESH)
-        return c
-
     def greet_plane(k, c):
         pl.semaphore_signal(barrier, inc=1, device_id=in_plane(k)[1], device_id_type=MESH)
         return c
 
-    lax.fori_loop(1, nz, greet_line, 0)
+    reach = nz // 4
+    for k in range(1, reach + 1):
+        for way in (k, nz - k):
+            pl.semaphore_signal(barrier, inc=1, device_id=in_line(way), device_id_type=MESH)
     lax.fori_loop(1, planes, greet_plane, 0)
     sides = [(-1, 0), (1, 0), (0, -1), (0, 1), (-1, -1), (-1, 1), (1, -1), (1, 1)]
 
     def beside(side):
         return {"gx": (gx + side[0] + nx) % nx, "gy": (gy + side[1] + ny) % ny}
 
-    for side in sides:
+    for side in sides[:2] + sides[4:]:
         pl.semaphore_signal(barrier, inc=1, device_id=beside(side), device_id_type=MESH)
 
     pending = []
 
-    def send_line(buf, sem, rows):
+    def send_line(src, dst, sem, rows, scatter):
         def body(k, c):
             far_half = nz // 2 + ((k + 1) // 2) * (1 - 2 * (k % 2))
-            spot = buf.at[z, pl.ds(0, rows)]
+            peer = (z + far_half) % nz
             pltpu.make_async_remote_copy(
-                spot, spot, sem.at[0], sem.at[1], device_id=in_line(far_half), device_id_type=MESH
+                src.at[peer if scatter else z, pl.ds(0, rows)],
+                dst.at[z, pl.ds(0, rows)],
+                sem.at[0], sem.at[1], device_id=in_line(far_half), device_id_type=MESH,
             ).start()
             return c
 
         lax.fori_loop(0, nz - 1, body, 0)
-        pending.append((buf, sem, nz - 1, rows))
+        pending.append((src, sem, nz - 1, rows))
 
     def send_plane(src, dst, sem, rows, scatter):
         def body(k, c):
@@ -192,12 +193,14 @@
     quad_high, quad_low = split((quad2[:, :COEF] + quad2[:, COEF:])[0:8])
     pair = jnp.concatenate([quad_high.astype(f32), quad_low.astype(f32)], axis=0).astype(bf16)
     raised = dot(pair, up_high) + dot(pair, up_low)
-    ebuf[z, 0:4, :] = (raised[0:8] + raised[8:16])[0:4]
+    ebuf[spot_in_plane, 0:4, :] = (raised[0:8] + raised[8:16])[0:4]
     load_sample.wait()
     sampled = [basis[k, 0:SAMPLE, :] for k in range(KB)]
-    ebuf[z, 4:5, :] = to_lanes([fold(v * sampled[KB - 1]) for v in sampled])
-    pl.semaphore_wait(barrier, nz + planes + 6)
-    send_line(ebuf, e_sem, 5)
+    ebuf[spot_in_plane, 4:5, :] = to_lanes([fold(v * sampled[KB - 1]) for v in sampled])
+    pl.semaphore_wait(barrier, 2 * reach + planes - 1 + 6)
+    send_plane(ebuf, ebuf, e_sem, 5, False)
+    for i, way in enumerate((reach, nz - reach)):
+        pl.semaphore_signal(met.at[i], inc=1, device_id=in_line(way), device_id_type=MESH)
 
     member = jnp.concatenate(
         [ones_where(iota((BOXES, COEF), 0) == boxes[r : r + 1, :]) for r in range(SD // COEF)], axis=1
@@ -303,20 +306,22 @@
     near2 = dot(jnp.concatenate(highs, axis=1), mats)
     near = near2[:, :COEF] + near2[:, COEF:] + dot(jnp.concatenate(lows, axis=1), mat_high)
 
-    wait_all(ebuf, e_sem.at[1], nz - 1, 5)
+    wait_all(ebuf, e_sem.at[1], planes - 1, 5)
     blocks = ebuf[...]
-    sources = blocks.reshape(8 * nz, COEF)
+    sources = blocks.reshape(8 * planes, COEF)
     turned = pltpu.roll(times_i(sources), 4, 0)
     sources = jnp.where((iota(sources.shape, 0) & 4) == 0, sources, turned)
     source_high, source_low = split(sources)
     part2 = dot(far_w[0], jnp.concatenate([source_high, source_low], axis=1))
     part = part2[:, :COEF] + part2[:, COEF:] + dot(far_w[1], source_high)
     sample_sum = jnp.sum(blocks, axis=0)[4:5, :]
-    for j in range(planes):
+    for j in range(nz):
         pbuf[j, 0:4, :] = part[4 * j : 4 * j + 4]
         pbuf[j, 4:5, :] = sample_sum
-    rbuf[spot_in_plane, 0:5, :] = pbuf[spot_in_plane, 0:5, :]
-    send_plane(pbuf, rbuf, r_sem, 5, True)
+    rbuf[z, 0:5, :] = pbuf[z, 0:5, :]
+    for i in range(2):
+        pl.semaphore_wait(met.at[i], 1)
+    send_line(pbuf, rbuf, r_sem, 5, True)
 
     near_pair = jnp.concatenate(split(near), axis=1)
     for r in range(SD // CHUNK):
@@ -330,7 +335,7 @@
             value = jnp.where(own_type == t, all_types[:, t * COEF : (t + 1) * COEF], value)
         image[rows, :] = basis[KB - 1, rows, :] - value
 
-    wait_all(rbuf, r_sem.at[1], planes - 1, 5)
+    wait_all(rbuf, r_sem.at[1], nz - 1, 5)
     arrived = jnp.sum(rbuf[...], axis=0)
     far = jnp.where(iota((8, COEF), 0) < 4, arrived, 0.0)
     sample_row = arrived[4:5, :]
@@ -356,7 +361,7 @@
         sums[KB] = sums[KB] + fold(w * w)
 
     abuf[z, 0:1, :] = to_lanes(sums + grams)
-    send_line(abuf, a_sem, 1)
+    send_line(abuf, abuf, a_sem, 1, False)
     wait_all(abuf, a_sem.at[1], nz - 1, 1)
     bbuf[spot_in_plane, 0:1, :] = jnp.sum(abuf[...], axis=0)
     send_plane(bbuf, bbuf, b_sem, 1, False)
@@ -384,7 +389,6 @@
     beta = jnp.sqrt(jnp.maximum(square, 0.0) / count + 1e-06)
     scale = 1.0 / beta
 
-    outs = []
     for r in range(SD // CHUNK):
         rows = pl.ds(r * CHUNK, CHUNK)
         w = image[rows, :]
@@ -397,8 +401,6 @@
         copy.wait_send()
     for buf, sem, number, rows in pending:
         wait_all(buf, sem.at[0], number, rows)
-    for copy in outs:
-        copy.wait()
 
 
 def on_device(nx, ny, basis, sphere_box, sphere_type, near_offsets, near_mats, up_mat, top_mat, tmats, bloch_angle):
@@ -419,9 +421,9 @@
             vmem((COEF, COEF), f32),
             vmem((NTYPE, COEF, COEF), f32),
             pltpu.SMEM((2,), f32),
+            vmem((2 * ny, 8, COEF), f32),
             vmem((nz, 8, COEF), f32),
-            vmem((2 * ny, 8, COEF), f32),
-            vmem((2 * ny, 8, COEF), f32),
+            vmem((nz, 8, COEF), f32),
             vmem((nz, 1, COEF), f32),
             vmem((2 * ny, 1, COEF), f32),
             vmem((4, LX, COEF), f32),
@@ -429,7 +431,7 @@
             vmem((4, LX, COEF), f32),
             vmem((4, 1, COEF), f32),
             vmem((LX + 2, LY + 16, COEF), f32),
-            vmem((2, 8 * ny, 8 * nz), bf16),
+            vmem((2, 4 * nz, 16 * ny), bf16),
             vmem((2, COEF, NTYPE * COEF), bf16),
             vmem((SD, COEF), bf16),
             vmem((SD, BOXES), bf16),
@@ -442,7 +444,7 @@
             dma((2,)),
             dma((8,)),
             dma((8,)),
-            dma((SD // CHUNK,)),
+            pltpu.SemaphoreType.REGULAR((2,)),
         ],
         compiler_params=pltpu.CompilerParams(
             collective_id=0, has_side_effects=True, vmem_limit_bytes=48 * 1024 * 1024

time: 44.6 us -> 43.3 us (0.971)
  Pallas kernels: 42.6 us -> 41.2 us
    pallas_call x1, Pallas kernels: 42.6 us -> 41.2 us  [on_device(): pl.pallas_call(functools.partial(kernel, nx, ny), out_shape=(pltpu.VMEM((...]
where the time goes in v4:
time: 43.3 us; the launch traced here: 43.1 us
  Pallas kernels  41.2 us (95%)
  local copies, waits for them, and re-layouts  1.31 us (3%)
  between operations  0.64 us (1%)
    pallas_call x1, Pallas kernels, on_device(): pl.pallas_call(functools.partial(kernel, nx, ny), out_shape=(pltpu.VMEM((...  41.2 us
    unnamed x2, local copies, waits for them, and re-layouts  1.31 us

profile of v4, /device:TPU:1, one launch (start us, length us, event | category | flops | bytes accessed | tf_op | source)
XLA Modules:
  0.0 43.1 jit_solution(8813270006318867199)
XLA Ops:
  0.6 41.2 %arnoldi_step.1 = (f32[1024,128]{1,0:T(8,128)S(1)}, f32[4]{0:T(128)S(4)}) custom-call(f32[3,1024,128]{2,1,0:T(8,128)} %basis_in.1, s32[8,128]{1,0:T(8,128)} %bitcast.3, s32[8,128]{1,0:T(8,128)} %bitcast.4, s32[2,9]{1,0:T(2,128)} %bitcast.5, f32[9,128,128]{2,1,0:T(8,128)} %near_in.1, f32[128,128]{1,0:T(8,128)} %up_in.1, f32[128,128]{1,0:T(8,128)} %top_in.1, ...), custom_call_target="tpu_custom_call" | custom-call | tf_op jit(solution)/shard_map/arnoldi_step/pallas_call | solution.py:409
  41.8 0.8 %copy.13 = f32[1024,128]{1,0:T(8,128)} copy(f32[1024,128]{1,0:T(8,128)S(1)} %get-tuple-element.2) | data formatting | bytes 1048576
  42.6 0.5 %copy.14 = f32[4]{0:T(128)} copy(f32[4]{0:T(128)S(4)} %get-tuple-element.3) | data formatting | bytes 32

commit v5 on v4

--- a/solution.py
+++ b/solution.py
@@ -51,12 +51,12 @@
     return jnp.sum(jnp.where(iota(x.shape, 1) == lane, x, 0.0), axis=1, keepdims=True)
 
 
-def to_lanes(parts):
+def to_lanes(parts, first=0):
     size = -(-len(parts) // 8) * 8
     rows = [jnp.sum(p, axis=0, keepdims=True) for p in parts]
     rows += [jnp.zeros((size - len(rows), COEF), f32)]
     sums = jnp.sum(jnp.concatenate(rows, axis=0), axis=1, keepdims=True)
-    placed = jnp.where(iota((size, COEF), 0) == iota((size, COEF), 1), sums, 0.0)
+    placed = jnp.where(iota((size, COEF), 0) + first == iota((size, COEF), 1), sums, 0.0)
     return jnp.sum(placed, axis=0, keepdims=True)
 
 
@@ -106,6 +106,32 @@
         copy.start()
         return copy
 
+    barrier = pltpu.get_barrier_semaphore()
+
+    def in_line(k):
+        return {"gx": half * nz + (z + k) % nz}
+
+    def in_plane(k):
+        peer = (spot_in_plane + k) % planes
+        return peer, {"gx": (peer // ny) * nz + z, "gy": peer % ny}
+
+    def greet_plane(k, c):
+        pl.semaphore_signal(barrier, inc=1, device_id=in_plane(k)[1], device_id_type=MESH)
+        return c
+
+    reach = nz // 4
+    for k in range(1, reach + 1):
+        for way in (k, nz - k):
+            pl.semaphore_signal(barrier, inc=1, device_id=in_line(way), device_id_type=MESH)
+    lax.fori_loop(1, planes, greet_plane, 0)
+    sides = [(-1, 0), (1, 0), (0, -1), (0, 1), (-1, -1), (-1, 1), (1, -1), (1, 1)]
+
+    def beside(side):
+        return {"gx": (gx + side[0] + nx) % nx, "gy": (gy + side[1] + ny) % ny}
+
+    for side in sides[:2] + sides[4:]:
+        pl.semaphore_signal(barrier, inc=1, device_id=beside(side), device_id_type=MESH)
+
     load_vec = load(basis_in.at[KB - 1], basis.at[KB - 1], 0)
     load_box = load(box_in, box, 1)
     load_up = load(up_in, up, 2)
@@ -119,32 +145,6 @@
     load_tmats = load(tmats_in, tmats, 9)
     rest = pl.ds(SAMPLE, SD - SAMPLE)
     load_basis = load(basis_in.at[others, rest], basis.at[others, rest], 10)
-
-    barrier = pltpu.get_barrier_semaphore()
-
-    def in_line(k):
-        return {"gx": half * nz + (z + k) % nz}
-
-    def in_plane(k):
-        peer = (spot_in_plane + k) % planes
-        return peer, {"gx": (peer // ny) * nz + z, "gy": peer % ny}
-
-    def greet_plane(k, c):
-        pl.semaphore_signal(barrier, inc=1, device_id=in_plane(k)[1], device_id_type=MESH)
-        return c
-
-    reach = nz // 4
-    for k in range(1, reach + 1):
-        for way in (k, nz - k):
-            pl.semaphore_signal(barrier, inc=1, device_id=in_line(way), device_id_type=MESH)
-    lax.fori_loop(1, planes, greet_plane, 0)
-    sides = [(-1, 0), (1, 0), (0, -1), (0, 1), (-1, -1), (-1, 1), (1, -1), (1, 1)]
-
-    def beside(side):
-        return {"gx": (gx + side[0] + nx) % nx, "gy": (gy + side[1] + ny) % ny}
-
-    for side in sides[:2] + sides[4:]:
-        pl.semaphore_signal(barrier, inc=1, device_id=beside(side), device_id_type=MESH)
 
     pending = []
 
@@ -228,16 +228,34 @@
         halo.append(copy)
     pad[1 : LX + 1, 8 : 8 + LY, :] = leaf
 
+    load_bloch.wait()
+    theta = (bloch[0], bloch[1])
+    weights = far_weights(nx, ny, nz, gx, gy, theta)
+    far_w[0], far_w[1] = split(weights)
+
+    wait_all(ebuf, e_sem.at[1], planes - 1, 5)
+    blocks = ebuf[...]
+    sources = blocks.reshape(8 * planes, COEF)
+    turned = pltpu.roll(times_i(sources), 4, 0)
+    sources = jnp.where((iota(sources.shape, 0) & 4) == 0, sources, turned)
+    source_high, source_low = split(sources)
+    part2 = dot(far_w[0], jnp.concatenate([source_high, source_low], axis=1))
+    part = part2[:, :COEF] + part2[:, COEF:] + dot(far_w[1], source_high)
+    sample_sum = jnp.sum(blocks, axis=0)[4:5, :]
+    for j in range(nz):
+        pbuf[j, 0:4, :] = part[4 * j : 4 * j + 4]
+        pbuf[j, 4:5, :] = sample_sum
+    rbuf[z, 0:5, :] = pbuf[z, 0:5, :]
+    for i in range(2):
+        pl.semaphore_wait(met.at[i], 1)
+    send_line(pbuf, rbuf, r_sem, 5, True)
+
     load_basis.wait()
     grams = []
     for j in range(KB):
         for k in range(j, KB):
             grams.append(fold(basis[j] * basis[k]))
-
-    load_bloch.wait()
-    theta = (bloch[0], bloch[1])
-    weights = far_weights(nx, ny, nz, gx, gy, theta)
-    far_w[0], far_w[1] = split(weights)
+    gram_lanes = to_lanes(grams, KB + 1)
 
     load_type.wait()
     codes = boxes + BOXES * kind[...]
@@ -306,23 +324,6 @@
     near2 = dot(jnp.concatenate(highs, axis=1), mats)
     near = near2[:, :COEF] + near2[:, COEF:] + dot(jnp.concatenate(lows, axis=1), mat_high)
 
-    wait_all(ebuf, e_sem.at[1], planes - 1, 5)
-    blocks = ebuf[...]
-    sources = blocks.reshape(8 * planes, COEF)
-    turned = pltpu.roll(times_i(sources), 4, 0)
-    sources = jnp.where((iota(sources.shape, 0) & 4) == 0, sources, turned)
-    source_high, source_low = split(sources)
-    part2 = dot(far_w[0], jnp.concatenate([source_high, source_low], axis=1))
-    part = part2[:, :COEF] + part2[:, COEF:] + dot(far_w[1], source_high)
-    sample_sum = jnp.sum(blocks, axis=0)[4:5, :]
-    for j in range(nz):
-        pbuf[j, 0:4, :] = part[4 * j : 4 * j + 4]
-        pbuf[j, 4:5, :] = sample_sum
-    rbuf[z, 0:5, :] = pbuf[z, 0:5, :]
-    for i in range(2):
-        pl.semaphore_wait(met.at[i], 1)
-    send_line(pbuf, rbuf, r_sem, 5, True)
-
     near_pair = jnp.concatenate(split(near), axis=1)
     for r in range(SD // CHUNK):
         rows = pl.ds(r * CHUNK, CHUNK)
@@ -360,13 +361,13 @@
             sums[k] = sums[k] + fold(vectors[k] * w)
         sums[KB] = sums[KB] + fold(w * w)
 
-    abuf[z, 0:1, :] = to_lanes(sums + grams)
+    bbuf[spot_in_plane, 0:1, :] = to_lanes(sums) + gram_lanes
+    send_plane(bbuf, bbuf, b_sem, 1, False)
+    wait_all(bbuf, b_sem.at[1], planes - 1, 1)
+    abuf[z, 0:1, :] = jnp.sum(bbuf[...], axis=0)
     send_line(abuf, abuf, a_sem, 1, False)
     wait_all(abuf, a_sem.at[1], nz - 1, 1)
-    bbuf[spot_in_plane, 0:1, :] = jnp.sum(abuf[...], axis=0)
-    send_plane(bbuf, bbuf, b_sem, 1, False)
-    wait_all(bbuf, b_sem.at[1], planes - 1, 1)
-    totals = jnp.sum(bbuf[...], axis=0)
+    totals = jnp.sum(abuf[...], axis=0)
     inner = [total_lane(totals, k) for k in range(KB)]
     square = total_lane(totals, KB)
     gram, lane = {}, KB + 1

time: 43.3 us -> 42.3 us (0.977)
  Pallas kernels: 41.2 us -> 40.2 us
    pallas_call x1, Pallas kernels: 41.2 us -> 40.2 us  [on_device(): pl.pallas_call(functools.partial(kernel, nx, ny), out_shape=(pltpu.VMEM((...]
where the time goes in v5:
time: 42.3 us; the launch traced here: 42.2 us
  Pallas kernels  40.2 us (95%)
  local copies, waits for them, and re-layouts  1.31 us (3%)
  between operations  0.64 us (2%)
    pallas_call x1, Pallas kernels, on_device(): pl.pallas_call(functools.partial(kernel, nx, ny), out_shape=(pltpu.VMEM((...  40.2 us
    unnamed x2, local copies, waits for them, and re-layouts  1.31 us

profile of v5, /device:TPU:1, one launch (start us, length us, event | category | flops | bytes accessed | tf_op | source)
XLA Modules:
  0.0 42.2 jit_solution(12247020031382345255)
XLA Ops:
  0.6 40.2 %arnoldi_step.1 = (f32[1024,128]{1,0:T(8,128)S(1)}, f32[4]{0:T(128)S(4)}) custom-call(f32[3,1024,128]{2,1,0:T(8,128)} %basis_in.1, s32[8,128]{1,0:T(8,128)} %bitcast.3, s32[8,128]{1,0:T(8,128)} %bitcast.4, s32[2,9]{1,0:T(2,128)} %bitcast.5, f32[9,128,128]{2,1,0:T(8,128)} %near_in.1, f32[128,128]{1,0:T(8,128)} %up_in.1, f32[128,128]{1,0:T(8,128)} %top_in.1, ...), custom_call_target="tpu_custom_call" | custom-call | tf_op jit(solution)/shard_map/arnoldi_step/pallas_call | solution.py:410
  40.8 0.8 %copy.13 = f32[1024,128]{1,0:T(8,128)} copy(f32[1024,128]{1,0:T(8,128)S(1)} %get-tuple-element.2) | data formatting | bytes 1048576
  41.6 0.5 %copy.14 = f32[4]{0:T(128)} copy(f32[4]{0:T(128)S(4)} %get-tuple-element.3) | data formatting | bytes 32

commit v6 on v5

--- a/solution.py
+++ b/solution.py
@@ -16,7 +16,6 @@
 NOFF = 9
 BOXES = LX * LY
 CHUNK = 256
-SAMPLE = 128
 
 MESH = pl.DeviceIdType.MESH
 wave_number = 2.3
@@ -137,14 +136,12 @@
     load_up = load(up_in, up, 2)
     load_bloch = load(bloch_in, bloch, 3)
     others = pl.ds(0, KB - 1)
-    load_sample = load(basis_in.at[others, pl.ds(0, SAMPLE)], basis.at[others, pl.ds(0, SAMPLE)], 4)
+    load_basis = load(basis_in.at[others], basis.at[others], 4)
     load_type = load(type_in, kind, 5)
     load_offsets = load(offsets_in, offsets, 6)
     load_near = load(near_in, near_mats, 7)
     load_top = load(top_in, top, 8)
     load_tmats = load(tmats_in, tmats, 9)
-    rest = pl.ds(SAMPLE, SD - SAMPLE)
-    load_basis = load(basis_in.at[others, rest], basis.at[others, rest], 10)
 
     pending = []
 
@@ -194,11 +191,8 @@
     pair = jnp.concatenate([quad_high.astype(f32), quad_low.astype(f32)], axis=0).astype(bf16)
     raised = dot(pair, up_high) + dot(pair, up_low)
     ebuf[spot_in_plane, 0:4, :] = (raised[0:8] + raised[8:16])[0:4]
-    load_sample.wait()
-    sampled = [basis[k, 0:SAMPLE, :] for k in range(KB)]
-    ebuf[spot_in_plane, 4:5, :] = to_lanes([fold(v * sampled[KB - 1]) for v in sampled])
     pl.semaphore_wait(barrier, 2 * reach + planes - 1 + 6)
-    send_plane(ebuf, ebuf, e_sem, 5, False)
+    send_plane(ebuf, ebuf, e_sem, 4, False)
     for i, way in enumerate((reach, nz - reach)):
         pl.semaphore_signal(met.at[i], inc=1, device_id=in_line(way), device_id_type=MESH)
 
@@ -233,22 +227,19 @@
     weights = far_weights(nx, ny, nz, gx, gy, theta)
     far_w[0], far_w[1] = split(weights)
 
-    wait_all(ebuf, e_sem.at[1], planes - 1, 5)
-    blocks = ebuf[...]
-    sources = blocks.reshape(8 * planes, COEF)
+    wait_all(ebuf, e_sem.at[1], planes - 1, 4)
+    sources = ebuf[...].reshape(8 * planes, COEF)
     turned = pltpu.roll(times_i(sources), 4, 0)
     sources = jnp.where((iota(sources.shape, 0) & 4) == 0, sources, turned)
     source_high, source_low = split(sources)
     part2 = dot(far_w[0], jnp.concatenate([source_high, source_low], axis=1))
     part = part2[:, :COEF] + part2[:, COEF:] + dot(far_w[1], source_high)
-    sample_sum = jnp.sum(blocks, axis=0)[4:5, :]
     for j in range(nz):
         pbuf[j, 0:4, :] = part[4 * j : 4 * j + 4]
-        pbuf[j, 4:5, :] = sample_sum
-    rbuf[z, 0:5, :] = pbuf[z, 0:5, :]
+    rbuf[z, 0:4, :] = pbuf[z, 0:4, :]
     for i in range(2):
         pl.semaphore_wait(met.at[i], 1)
-    send_line(pbuf, rbuf, r_sem, 5, True)
+    send_line(pbuf, rbuf, r_sem, 4, True)
 
     load_basis.wait()
     grams = []
@@ -270,6 +261,18 @@
         spot = own_type * 8 + ((own_box >> 7) & 1) * 2 + ((own_box >> 3) & 1)
         hot[rows, :] = ones_where(spot == (lane & 63))
         field[rows, :] = own_type
+
+    spots = kind[...] * 8 + quarters
+    hot_t = jnp.concatenate(
+        [ones_where(iota((8 * NTYPE, COEF), 0) == spots[r : r + 1, :]) for r in range(SD // COEF)], axis=1
+    )
+    numbers = jnp.sum(hot_t.astype(f32), axis=1, keepdims=True)
+
+    def class_sums(x):
+        both = dot(hot_t, jnp.concatenate(split(x), axis=1))
+        return both[:, :COEF] + both[:, COEF:]
+
+    basis_sums = [class_sums(basis[k]) for k in range(KB)]
 
     load_top.wait()
     load_tmats.wait()
@@ -334,35 +337,28 @@
         value = all_types[:, :COEF]
         for t in range(1, NTYPE):
             value = jnp.where(own_type == t, all_types[:, t * COEF : (t + 1) * COEF], value)
-        image[rows, :] = basis[KB - 1, rows, :] - value
-
-    wait_all(rbuf, r_sem.at[1], nz - 1, 5)
+        image[rows, :] = -value
+
+    near_sums = [fold(basis[k] * image[...]) for k in range(KB)] + [fold(image[...] * image[...])]
+    near_class = class_sums(image[...])
+
+    wait_all(rbuf, r_sem.at[1], nz - 1, 4)
     arrived = jnp.sum(rbuf[...], axis=0)
     far = jnp.where(iota((8, COEF), 0) < 4, arrived, 0.0)
-    sample_row = arrived[4:5, :]
     far_high, far_low = split(far)
     far_pair = jnp.concatenate([far_high.astype(f32), far_low.astype(f32)], axis=0).astype(bf16)
     table2 = dot(far_pair, top_t[0]) + dot(far_pair, top_t[1])
     table = table2[0:8] + table2[8:16]
     table = jnp.concatenate([table[:, t * COEF : (t + 1) * COEF] for t in range(NTYPE)], axis=0)
+    sums = [near_sums[k] - fold(table * basis_sums[k]) for k in range(KB)]
+    sums.append(near_sums[KB] + fold(table * (table * numbers - 2.0 * near_class)))
+
+    bbuf[spot_in_plane, 0:1, :] = to_lanes(sums) + gram_lanes
+    send_plane(bbuf, bbuf, b_sem, 1, False)
     table = jnp.concatenate(split(table), axis=0)
-
-    sample_count = float(nx * ny * SAMPLE * COEF)
-    guess = [total_lane(sample_row, k) / sample_count for k in range(KB)]
-    sums = [jnp.zeros((8, COEF), f32)] * (KB + 1)
     for r in range(SD // CHUNK):
         rows = pl.ds(r * CHUNK, CHUNK)
-        w = image[rows, :] - dot(hot[rows, :], table)
-        vectors = [basis[k, rows, :] for k in range(KB)]
-        for k in range(KB):
-            w = w - guess[k] * vectors[k]
-        image[rows, :] = w
-        for k in range(KB):
-            sums[k] = sums[k] + fold(vectors[k] * w)
-        sums[KB] = sums[KB] + fold(w * w)
-
-    bbuf[spot_in_plane, 0:1, :] = to_lanes(sums) + gram_lanes
-    send_plane(bbuf, bbuf, b_sem, 1, False)
+        image[rows, :] = image[rows, :] - dot(hot[rows, :], table)
     wait_all(bbuf, b_sem.at[1], planes - 1, 1)
     abuf[z, 0:1, :] = jnp.sum(bbuf[...], axis=0)
     send_line(abuf, abuf, a_sem, 1, False)
@@ -375,13 +371,8 @@
         for k in range(j, KB):
             gram[j, k] = gram[k, j] = total_lane(totals, lane)
             lane += 1
-    coeffs = []
-    for k in range(KB):
-        value = inner[k]
-        for j in range(KB):
-            value = value + gram[k, j] * guess[j]
-        coeffs.append(value / count)
-    step = [coeffs[k] - guess[k] for k in range(KB)]
+    coeffs = [(inner[k] + gram[k, KB - 1]) / count for k in range(KB)]
+    step = [coeffs[k] - (1.0 if k == KB - 1 else 0.0) for k in range(KB)]
     for k in range(KB):
         along = -2.0 * inner[k]
         for j in range(KB):
@@ -438,7 +429,7 @@
             vmem((SD, BOXES), bf16),
             vmem((SD, COEF), f32),
             vmem((SD, COEF), i32),
-            dma((11,)),
+            dma((10,)),
             dma((2,)),
             dma((2,)),
             dma((2,)),

time: 42.3 us -> 41.8 us (0.988)
  Pallas kernels: 40.2 us -> 39.7 us
    pallas_call x1, Pallas kernels: 40.2 us -> 39.7 us  [on_device(): pl.pallas_call(functools.partial(kernel, nx, ny), out_shape=(pltpu.VMEM((...]
where the time goes in v6:
time: 41.8 us; the launch traced here: 41.6 us
  Pallas kernels  39.7 us (95%)
  local copies, waits for them, and re-layouts  1.31 us (3%)
  between operations  0.64 us (2%)
    pallas_call x1, Pallas kernels, on_device(): pl.pallas_call(functools.partial(kernel, nx, ny), out_shape=(pltpu.VMEM((...  39.7 us
    unnamed x2, local copies, waits for them, and re-layouts  1.31 us

profile of v6, /device:TPU:1, one launch (start us, length us, event | category | flops | bytes accessed | tf_op | source)
XLA Modules:
  0.0 41.6 jit_solution(10064332791136681113)
XLA Ops:
  0.6 39.7 %arnoldi_step.1 = (f32[1024,128]{1,0:T(8,128)S(1)}, f32[4]{0:T(128)S(4)}) custom-call(f32[3,1024,128]{2,1,0:T(8,128)} %basis_in.1, s32[8,128]{1,0:T(8,128)} %bitcast.3, s32[8,128]{1,0:T(8,128)} %bitcast.4, s32[2,9]{1,0:T(2,128)} %bitcast.5, f32[9,128,128]{2,1,0:T(8,128)} %near_in.1, f32[128,128]{1,0:T(8,128)} %up_in.1, f32[128,128]{1,0:T(8,128)} %top_in.1, ...), custom_call_target="tpu_custom_call" | custom-call | tf_op jit(solution)/shard_map/arnoldi_step/pallas_call | solution.py:401
  40.3 0.8 %copy.13 = f32[1024,128]{1,0:T(8,128)} copy(f32[1024,128]{1,0:T(8,128)S(1)} %get-tuple-element.2) | data formatting | bytes 1048576
  41.1 0.5 %copy.14 = f32[4]{0:T(128)} copy(f32[4]{0:T(128)S(4)} %get-tuple-element.3) | data formatting | bytes 32

commit v7 on v6

--- a/solution.py
+++ b/solution.py
@@ -161,7 +161,7 @@
 
     def send_plane(src, dst, sem, rows, scatter):
         def body(k, c):
-            peer, device = in_plane(k)
+            peer, device = in_plane(1 + (k + planes // 2 + ny // 2 - 2) % (planes - 1))
             pltpu.make_async_remote_copy(
                 src.at[peer if scatter else spot_in_plane, pl.ds(0, rows)],
                 dst.at[spot_in_plane, pl.ds(0, rows)],
@@ -381,14 +381,14 @@
     beta = jnp.sqrt(jnp.maximum(square, 0.0) / count + 1e-06)
     scale = 1.0 / beta
 
+    for k, value in enumerate(coeffs + [beta]):
+        hess_ref[k] = jnp.sum(value)
     for r in range(SD // CHUNK):
         rows = pl.ds(r * CHUNK, CHUNK)
         w = image[rows, :]
         for k in range(KB):
             w = w - step[k] * basis[k, rows, :]
         out_ref[rows, :] = w * scale
-    for k, value in enumerate(coeffs + [beta]):
-        hess_ref[k] = jnp.sum(value)
     for copy in halo:
         copy.wait_send()
     for buf, sem, number, rows in pending:

time: 41.8 us -> 41.8 us (level)
  no operation moved by 1% of the time
where the time goes in v7:
time: 41.8 us; the launch traced here: 41.7 us
  Pallas kernels  39.8 us (95%)
  local copies, waits for them, and re-layouts  1.31 us (3%)
  between operations  0.64 us (2%)
    pallas_call x1, Pallas kernels, on_device(): pl.pallas_call(functools.partial(kernel, nx, ny), out_shape=(pltpu.VMEM((...  39.8 us
    unnamed x2, local copies, waits for them, and re-layouts  1.31 us

profile of v7, /device:TPU:1, one launch (start us, length us, event | category | flops | bytes accessed | tf_op | source)
XLA Modules:
  0.0 41.7 jit_solution(7175547444886403036)
XLA Ops:
  0.6 39.8 %arnoldi_step.1 = (f32[1024,128]{1,0:T(8,128)S(1)}, f32[4]{0:T(128)S(4)}) custom-call(f32[3,1024,128]{2,1,0:T(8,128)} %basis_in.1, s32[8,128]{1,0:T(8,128)} %bitcast.3, s32[8,128]{1,0:T(8,128)} %bitcast.4, s32[2,9]{1,0:T(2,128)} %bitcast.5, f32[9,128,128]{2,1,0:T(8,128)} %near_in.1, f32[128,128]{1,0:T(8,128)} %up_in.1, f32[128,128]{1,0:T(8,128)} %top_in.1, ...), custom_call_target="tpu_custom_call" | custom-call | tf_op jit(solution)/shard_map/arnoldi_step/pallas_call | solution.py:401
  40.4 0.8 %copy.13 = f32[1024,128]{1,0:T(8,128)} copy(f32[1024,128]{1,0:T(8,128)S(1)} %get-tuple-element.2) | data formatting | bytes 1048576
  41.2 0.5 %copy.14 = f32[4]{0:T(128)} copy(f32[4]{0:T(128)S(4)} %get-tuple-element.3) | data formatting | bytes 32
